TPU v7x, 256 devices: a whole 4x4x8 slice. The times are simulated.
256 devices in a mesh: dp: 64 (over y, x_lo, z), feat: 4 (over x_hi, core).
Axes of the slice: x: 4 (x_hi: 2, x_lo: 2; x = x_hi * 2 + x_lo), y: 4, z: 8, core: 2. Of those that a mesh axis runs over, the one named last changes fastest.
Arguments:
- embed_a: bfloat16 [16384, 4096], P('dp', 'feat'), may hold values from -300 to 300
- embed_b: bfloat16 [16384, 4096], P('dp', 'feat'), may hold values from -300 to 300
Outputs:
- grad_a: bfloat16 [16384, 4096], P('dp', 'feat')
- grad_b: bfloat16 [16384, 4096], P('dp', 'feat')
- loss_mean: float32 [], replicated
All inputs are finite; a program needn't handle non-finite values.
Results may differ from a plain program's by a relative error of at most 0.008.
Values may be sent and summed in bfloat16 or wider, within the bound.
No kernel may reach another device: no remote copies, remote signals or barrier semaphores. Data moves between devices by JAX's collectives and lax.ppermute only.
A program may use at most 64 MiB of HBM per device.

v0:
```python
import jax
import jax.numpy as jnp
from jax import lax
from jax.sharding import PartitionSpec as P

off_weight = 0.0051
epsilon = 1e-05


def on_device(embed_a, embed_b):
    local_rows, feat_width = embed_a.shape
    groups = lax.axis_size("dp")
    batch_total = local_rows * groups
    full_width = feat_width * lax.axis_size("feat")
    own_rows = feat_width // groups
    value_a = embed_a.astype(jnp.float32)
    value_b = embed_b.astype(jnp.float32)
    sum_a, sum_b = lax.psum((jnp.sum(value_a, 0), jnp.sum(value_b, 0)), "dp")
    mean_a = sum_a / batch_total
    mean_b = sum_b / batch_total
    centred_a = value_a - mean_a
    centred_b = value_b - mean_b
    square_a, square_b = lax.psum(
        (jnp.sum(centred_a * centred_a, 0), jnp.sum(centred_b * centred_b, 0)), "dp"
    )
    var_a = square_a / batch_total
    var_b = square_b / batch_total
    scale_a = lax.rsqrt(var_a + epsilon)
    scale_b = lax.rsqrt(var_b + epsilon)
    norm_a = (centred_a * scale_a).astype(jnp.bfloat16)
    norm_b = (centred_b * scale_b).astype(jnp.bfloat16)
    full_b = lax.all_gather(norm_b, "feat", axis=1, tiled=True)
    first_row = lax.axis_index("feat") * feat_width + lax.axis_index("dp") * own_rows
    left_cols = norm_a
    cross_corr = (
        lax.psum_scatter(
            lax.dot_general(
                left_cols, full_b, (((0,), (0,)), ((), ())), preferred_element_type=jnp.float32
            ),
            "dp",
            scatter_dimension=0,
            tiled=True,
        )
        / batch_total
    )
    block_width = cross_corr.shape[1]
    row_ids = first_row + lax.broadcasted_iota(jnp.int32, (own_rows, block_width), 0)
    col_ids = lax.broadcasted_iota(jnp.int32, (own_rows, block_width), 1)
    diagonal = row_ids == col_ids
    loss_piece = jnp.sum(
        jnp.where(diagonal, (1.0 - cross_corr) ** 2, off_weight * cross_corr * cross_corr)
    )
    slope_piece = jnp.where(
        diagonal, 2.0 * (cross_corr - 1.0), 2.0 * off_weight * cross_corr
    ).astype(jnp.bfloat16)
    shard_rows = lax.all_gather(slope_piece, "dp", axis=0, tiled=True)
    new_a = lax.dot_general(
        full_b, shard_rows, (((1,), (1,)), ((), ())), preferred_element_type=jnp.float32
    )
    left_cols = norm_a
    part_cols = jnp.dot(left_cols, shard_rows, preferred_element_type=jnp.float32)
    loss_total = lax.psum(loss_piece, ("dp", "feat"))
    back_b = lax.psum_scatter(part_cols, "feat", scatter_dimension=1, tiled=True)
    plain_a = norm_a.astype(jnp.float32)
    plain_b = norm_b.astype(jnp.float32)
    one_a, two_a, one_b, two_b = lax.psum(
        (
            jnp.sum(new_a, 0),
            jnp.sum(new_a * plain_a, 0),
            jnp.sum(back_b, 0),
            jnp.sum(back_b * plain_b, 0),
        ),
        "dp",
    )
    grad_a = ((new_a - one_a / batch_total - plain_a * (two_a / batch_total)) * scale_a).astype(
        jnp.bfloat16
    )
    grad_b = ((back_b - one_b / batch_total - plain_b * (two_b / batch_total)) * scale_b).astype(
        jnp.bfloat16
    )
    return (grad_a, grad_b, loss_total / full_width)


def solution(mesh):
    placed = (P("dp", "feat"), P("dp", "feat"))
    return jax.shard_map(
        on_device,
        mesh=mesh,
        in_specs=placed,
        out_specs=(P("dp", "feat"), P("dp", "feat"), P()),
        check_vma=False,
    )
```

profile of v0, /device:TPU:4, one launch (start us, length us, event | category | flops | bytes accessed | tf_op | source)
XLA Modules:
  0.0 1433.7 jit_solution(8110274789342607517)
XLA Ops:
  7.2 0.0 all-gather.3.cloned.1.call-start
  7.2 1.1 convert_reduce_fusion
  8.3 1.1 convert_reduce_fusion.1
  9.5 163.3 %all-reduce.2 = (f32[1024]{0:T(1024)S(1)}, f32[1024]{0:T(1024)S(1)}) all-reduce(f32[1024]{0:T(1024)S(1)} %convert_reduce_fusion.1, f32[1024]{0:T(1024)S(1)} %convert_reduce_fusion), channel_id=1, replica_groups=mesh['dp'=64,'feat'=4] {'dp'}, use_global_device_ids=true, to_apply=%region_1.0 | all-reduce | flops 2048 | bytes 16384 | tf_op jit(solution)/shard_map/psum | solution.py:18
  172.8 1.2 fusion.4
  174.0 1.2 fusion.6
  175.2 154.4 %all-reduce.1 = (f32[1024]{0:T(1024)S(1)}, f32[1024]{0:T(1024)S(1)}) all-reduce(f32[1024]{0:T(1024)S(1)} %fusion.6, f32[1024]{0:T(1024)S(1)} %fusion.4), channel_id=1, replica_groups=mesh['dp'=64,'feat'=4] {'dp'}, use_global_device_ids=true, to_apply=%region_3.0 | all-reduce | flops 2048 | bytes 16384 | tf_op jit(solution)/shard_map/psum | solution.py:23
  329.6 2.0 fusion.7
  331.6 0.0 all-gather.3.cloned.1.call-update
  331.6 0.0 reduce-scatter.3.cloned.1.call-start
  331.7 21.7 %all-gather.3.cloned.1.call-done = bf16[256,4096]{1,0:T(8,128)(2,1)} async-done(((bf16[256,1024]{1,0:T(8,128)(2,1)}), bf16[256,4096]{1,0:T(8,128)(2,1)}) %all-gather.3.cloned.1.call-update) | async-done | bytes 2097168 | tf_op jit(solution)/shard_map/all_gather | solution.py:32
  353.4 9.9 fusion.21
  363.3 0.0 all-gather.5.cloned.1.call-start
  363.4 356.2 %reduce-scatter.3.cloned.1.call-done = f32[16,4096]{1,0:T(8,128)} async-done(((f32[1024,4096]{1,0:T(8,128)}), f32[16,4096]{1,0:T(8,128)}) %reduce-scatter.3.cloned.1.call-update) | async-done | bytes 262160 | tf_op jit(solution)/shard_map/reduce_scatter | solution.py:36
  719.6 2.3 select_reduce_fusion
  721.9 0.0 reduce-scatter.5.cloned.1.call-start
  722.0 305.5 %all-gather.5.cloned.1.call-done = bf16[1024,4096]{1,0:T(8,128)(2,1)} async-done(((bf16[16,4096]{1,0:T(8,128)(2,1)}), bf16[1024,4096]{1,0:T(8,128)(2,1)}) %all-gather.5.cloned.1.call-update) | async-done | bytes 8388624 | tf_op jit(solution)/shard_map/all_gather | solution.py:56
  1027.5 7.7 fusion.19
  1035.2 72.2 %psum.71 = f32[]{:T(128)} all-reduce(f32[]{:T(128)} %get-tuple-element.15), channel_id=1, replica_groups=mesh['dp'=64,'feat'=4] {'dp','feat'}, use_global_device_ids=true, to_apply=%region_19.20 | all-reduce | flops 1 | bytes 8 | tf_op jit(solution)/shard_map/psum | solution.py:62
  1108.1 6.7 fusion.24
  1114.8 1.5 fusion.23
  1116.3 305.1 %all-reduce = (f32[1024]{0:T(1024)S(1)}, f32[1024]{0:T(1024)S(1)}, f32[1024]{0:T(1024)S(1)}, f32[1024]{0:T(1024)S(1)}) all-reduce(f32[1024]{0:T(1024)S(1)} %get-tuple-element.6, f32[1024]{0:T(1024)S(1)} %get-tuple-element.5, f32[1024]{0:T(1024)S(1)} %get-tuple-element.4, ...), channel_id=1, replica_groups=mesh['dp'=64,'feat'=4] {'dp'}, use_global_device_ids=true, to_apply=%region_12.13 | all-reduce | flops 4096 | bytes 32768 | tf_op jit(solution)/shard_map/psum | solution.py:66
  1421.4 2.3 fusion.11
  1423.7 2.3 fusion.15
  (18 shorter events, 0.1 us)
Async XLA Ops:
  7.2 346.3 %all-gather.3.cloned.1.call-start = ((), (), s32[]{:S(2)}) async-start(), calls=%async_computation.2 | async-start | bytes 2621440 | tf_op jit(solution)/shard_map/all_gather | solution.py:32
  331.6 387.9 %reduce-scatter.3.cloned.1.call-start = ((), (), s32[]{:S(2)}) async-start(), calls=%async_computation.3 | async-start | bytes 17039360 | tf_op jit(solution)/shard_map/reduce_scatter | solution.py:36
  363.3 664.2 %copy-start = (bf16[256,1024]{1,0:T(8,128)(2,1)S(1)}, bf16[256,1024]{1,0:T(8,128)(2,1)}, u32[]{:S(2)}) copy-start(bf16[256,1024]{1,0:T(8,128)(2,1)} %param.2) | copy-start | bytes 1572868
  363.3 664.2 %all-gather.5.cloned.1.call-start = ((), (), s32[]{:S(2)}) async-start(), calls=%async_computation.4 | async-start | bytes 8519680 | tf_op jit(solution)/shard_map/all_gather | solution.py:56
  721.9 386.2 %copy-start.2 = (bf16[256,4096]{1,0:T(8,128)(2,1)S(1)}, bf16[256,4096]{1,0:T(8,128)(2,1)}, u32[]{:S(2)}) copy-start(bf16[256,4096]{1,0:T(8,128)(2,1)} %all-gather.3.cloned.1.call-done) | copy-start | bytes 6291460
  721.9 392.9 %reduce-scatter.5.cloned.1.call-start = ((), (), s32[]{:S(2)}) async-start(), calls=%async_computation.5 | async-start | bytes 5242880 | tf_op jit(solution)/shard_map/reduce_scatter | solution.py:63
  1035.2 79.6 %copy-start.1 = (bf16[256,1024]{1,0:T(8,128)(2,1)S(1)}, bf16[256,1024]{1,0:T(8,128)(2,1)}, u32[]{:S(2)}) copy-start(bf16[256,1024]{1,0:T(8,128)(2,1)} %param.3) | copy-start | bytes 1572868
Sparse Core Ops, SparseCore 0:
  331.8 21.6 all-gather.2
  363.4 356.0 reduce-scatter.2
  722.0 305.3 all-gather.4
  1035.3 51.2 reduce-scatter.4
where the time goes:
time: 1430 us
  blocking collectives  695 us (49%)
  waiting for transfers between devices  683 us (48%)
  matrix products  24.3 us (2%)
  between operations  15.6 us (1%)
  other arithmetic  15 us (1%)
    reduce_scatter x1, waiting for transfers between devices, on_device(): lax.psum_scatter(lax.dot_general(left_cols, full_b, (((0,), (0,)), ((), (...  356 us
    all_gather x1, waiting for transfers between devices, on_device(): shard_rows = lax.all_gather(slope_piece, 'dp', axis=0, tiled=True)  306 us
    psum x1, blocking collectives, on_device(): lax.psum((jnp.sum(new_a, 0), jnp.sum(new_a * plain_a, 0), jnp.sum(back_b,...  305 us
    psum x1, blocking collectives, on_device(): sum_a, sum_b = lax.psum((jnp.sum(value_a, 0), jnp.sum(value_b, 0)), 'dp')  163 us
    psum x1, blocking collectives, on_device(): lax.psum((jnp.sum(centred_a * centred_a, 0), jnp.sum(centred_b * centred_...  154 us
    psum x1, blocking collectives, on_device(): loss_total = lax.psum(loss_piece, ('dp', 'feat'))  72.2 us
  transfers between devices with their start and end apart: 4, of which 3 were waited for; matrix products, arithmetic and copies ran while one was open for 0% of the time, Pallas kernels for 0%

commit v1 on v0

v1 whole, which is shorter than its diff:
```python
import jax
import jax.numpy as jnp
from jax import lax
from jax.sharding import Mesh, PartitionSpec as P

off_weight = 0.0051
epsilon = 1e-05

PLANE = ("y", "xh", "co")
BATCH = ("xl", "z")
f32 = jnp.float32
bf16 = jnp.bfloat16


def swap(value, axis):
    return lax.ppermute(value, axis, [(0, 1), (1, 0)])


def butterfly(value, axis):
    size = lax.axis_size(axis)
    step = 1
    while step < size:
        value = value + lax.ppermute(value, axis, [(i, i ^ step) for i in range(size)])
        step *= 2
    return value


def transpose_blocks(value):
    pairs = [(g * 4 + f, f * 4 + g) for g in range(4) for f in range(4)]
    return lax.ppermute(value, PLANE, pairs)


def on_device(embed_a, embed_b):
    rows, width = embed_a.shape
    y, xl, z = lax.axis_index("y"), lax.axis_index("xl"), lax.axis_index("z")
    xh, co = lax.axis_index("xh"), lax.axis_index("co")
    parts = 16
    group_rows = rows * 4
    total = group_rows * parts
    full_width = width * 4

    with jax.named_scope("gather"):
        block_a = lax.all_gather(embed_a, "y", axis=0, tiled=True)
        mine = transpose_blocks(embed_b)
        theirs = swap(mine, "xh")
        pair = jnp.concatenate(
            [jnp.where(xh == 0, mine, theirs), jnp.where(xh == 0, theirs, mine)], 0
        )
        other = swap(pair, "co")
        even = jnp.where(co == 0, pair, other)
        odd = jnp.where(co == 0, other, pair)
        block_b = jnp.concatenate([even[:rows], odd[:rows], even[rows:], odd[rows:]], 0)

    with jax.named_scope("local_stats"):
        value_a = block_a.astype(f32)
        value_b = block_b.astype(f32)
        local_a = jnp.sum(value_a, 0) / group_rows
        local_b = jnp.sum(value_b, 0) / group_rows
        cent_a = value_a - local_a
        cent_b = value_b - local_b
        stats = jnp.stack(
            [
                local_a,
                jnp.sum(cent_a * cent_a, 0),
                local_b,
                jnp.sum(cent_b * cent_b, 0),
                jnp.sum(cent_a * cent_b, 0),
            ]
        )

    with jax.named_scope("corr"):
        product = lax.dot_general(
            cent_a.astype(bf16),
            cent_b.astype(bf16),
            (((0,), (0,)), ((), ())),
            preferred_element_type=f32,
        ).astype(bf16)
        summed = lax.psum_scatter(product, "z", scatter_dimension=0, tiled=True)
        half = summed.shape[0] // 2
        low, high = summed[:half], summed[half:]
        received = swap(jnp.where(xl == 0, high, low), "xl")
        piece = jnp.where(xl == 0, low, high).astype(f32) + received.astype(f32)

    with jax.named_scope("global_stats"):
        every = lax.all_gather(stats, BATCH)
        mean_a = jnp.sum(every[:, 0], 0) / parts
        mean_b = jnp.sum(every[:, 2], 0) / parts
        shift_a = every[:, 0] - mean_a
        shift_b = every[:, 2] - mean_b
        var_a = (jnp.sum(every[:, 1], 0) + group_rows * jnp.sum(shift_a * shift_a, 0)) / total
        var_b = (jnp.sum(every[:, 3], 0) + group_rows * jnp.sum(shift_b * shift_b, 0)) / total
        scale_a = lax.rsqrt(var_a + epsilon)
        scale_b = lax.rsqrt(var_b + epsilon)
        diag_corr = (
            (jnp.sum(every[:, 4], 0) + group_rows * jnp.sum(shift_a * shift_b, 0))
            / total
            * scale_a
            * scale_b
        )

    with jax.named_scope("norm"):
        norm_a = ((value_a - mean_a) * scale_a).astype(bf16)
        norm_b = ((value_b - mean_b) * scale_b).astype(bf16)
        plain_a = norm_a.astype(f32)
        plain_b = norm_b.astype(f32)
        norm_sums = jnp.stack([jnp.sum(plain_a, 0), jnp.sum(plain_b, 0)])

    with jax.named_scope("slope"):
        diagonal_block = y == xh * 2 + co
        first_row = z * (2 * half) + xl * half
        row_shift = lax.dynamic_slice_in_dim(shift_a, first_row, half, 1)
        row_scale = lax.dynamic_slice_in_dim(scale_a, first_row, half, 0)
        between = lax.dot_general(
            row_shift,
            shift_b,
            (((0,), (0,)), ((), ())),
            precision=lax.Precision.HIGHEST,
            preferred_element_type=f32,
        )
        corr = (piece + group_rows * between) * (row_scale[:, None] * (scale_b / total))
        row_ids = first_row + lax.broadcasted_iota(jnp.int32, corr.shape, 0)
        col_ids = lax.broadcasted_iota(jnp.int32, corr.shape, 1)
        diagonal = jnp.logical_and(row_ids == col_ids, diagonal_block)
        diag_slope = (2.0 * (diag_corr - 1.0)).astype(bf16)
        slope_piece = jnp.where(
            diagonal, diag_slope[None, :], (2.0 * off_weight * corr).astype(bf16)
        )
        loss_piece = jnp.sum(
            jnp.where(diagonal, (1.0 - diag_corr) ** 2, off_weight * corr * corr)
        )
        slope_other = swap(slope_piece, "xl")
        slope_pair = jnp.concatenate(
            [
                jnp.where(xl == 0, slope_piece, slope_other),
                jnp.where(xl == 0, slope_other, slope_piece),
            ],
            0,
        )
        slope = lax.all_gather(slope_pair, "z", axis=0, tiled=True)

    with jax.named_scope("small_sums"):
        small = jnp.concatenate([norm_sums, jnp.full((1, width), loss_piece)], 0)
        small = butterfly(butterfly(small, "xl"), "z")
        loss_total = small[2:3, :128]
        loss_total = butterfly(butterfly(butterfly(loss_total, "co"), "xh"), "y")
        loss_mean = loss_total[0, 0] / full_width
        centre_a = small[0:1] / total
        centre_b = small[1:2] / total

    with jax.named_scope("back"):
        wide = slope.astype(f32)
        eye = jnp.logical_and(
            lax.broadcasted_iota(jnp.int32, slope.shape, 0)
            == lax.broadcasted_iota(jnp.int32, slope.shape, 1),
            diagonal_block,
        )
        squares = jnp.where(eye, 0.0, wide * wide) / (2.0 * off_weight)
        diag_term = jnp.where(diagonal_block, diag_slope.astype(f32) * diag_corr, 0.0)
        two_a = jnp.sum(squares, 1) + diag_term
        two_b = jnp.sum(squares, 0) + diag_term
        one_a = jnp.sum(wide * centre_b, 1)
        one_b = jnp.sum(wide * centre_a.reshape(width, 1), 0)
        back_a = lax.dot_general(
            norm_b, slope, (((1,), (1,)), ((), ())), preferred_element_type=f32
        )
        part_a = ((back_a - one_a - plain_a * two_a) * scale_a).astype(bf16)
        back_b = jnp.dot(norm_a, slope, preferred_element_type=f32)
        part_b = ((back_b - one_b - plain_b * two_b) * scale_b).astype(bf16)

    with jax.named_scope("reduce"):
        grad_a = lax.psum_scatter(part_a, "y", scatter_dimension=0, tiled=True)
        quarters = part_b.reshape(2, 2, rows, width)
        even, odd = quarters[:, 0], quarters[:, 1]
        received = swap(jnp.where(co == 0, odd, even), "co")
        pair = jnp.where(co == 0, even, odd).astype(f32) + received.astype(f32)
        received = swap(jnp.where(xh == 0, pair[1], pair[0]).astype(bf16), "xh")
        mine = jnp.where(xh == 0, pair[0], pair[1]) + received.astype(f32)
        grad_b = transpose_blocks(mine.astype(bf16))
    return (grad_a, grad_b, loss_mean)


def solution(mesh):
    fine = Mesh(mesh.devices.reshape(4, 2, 8, 2, 2), ("y", "xl", "z", "xh", "co"))
    placed = P(("y", "xl", "z"), ("xh", "co"))
    return jax.shard_map(
        on_device,
        mesh=fine,
        in_specs=(placed, placed),
        out_specs=(placed, placed, P()),
        check_vma=False,
    )
```

time: 1430 us -> 228 us (0.16)
  blocking collectives: 695 us -> 42.2 us
  waiting for transfers between devices: 683 us -> 106 us
  starting transfers between devices: 0.16 us -> 20.3 us
    psum x4 -> x0, blocking collectives: 695 us -> none  [the longest x1 305 us: on_device(): lax.psum((jnp.sum(new_a, 0), jnp.sum(new_a * plain_a, 0), jnp.sum(back_b,...]
    reduce_scatter x2, waiting for transfers between devices: 356 us -> 0.02 us  [the longest x1 0.02 us: on_device(): grad_a = lax.psum_scatter(part_a, 'y', scatter_dimension=0, tiled=True)]
    all_gather x2, waiting for transfers between devices: 327 us -> 13.6 us  [the longest x1 13.6 us: on_device(): slope = lax.all_gather(slope_pair, 'z', axis=0, tiled=True)]
    ppermute x0 -> x16, waiting for transfers between devices: none -> 92.6 us  [the longest x6 42.7 us: swap(): return lax.ppermute(value, axis, [(0, 1), (1, 0)])]
    all_gather x0 -> x1, blocking collectives: none -> 42.2 us  [on_device(): every = lax.all_gather(stats, BATCH)]
    ppermute x0 -> x16, starting transfers between devices: none -> 20.1 us  [the longest x2 9.94 us: transpose_blocks(): return lax.ppermute(value, PLANE, pairs)]
  transfers between devices with their start and end apart: 4 -> 20, of which waited for: 3 -> 16; matrix products, arithmetic and copies ran while one was open for 0% -> 8% of each run, Pallas kernels for 0% -> 0%
where the time goes in v1:
time: 228 us; the launch traced here: 225 us
  waiting for transfers between devices  106 us (46%)
  blocking collectives  42.2 us (19%)
  starting transfers between devices  20.3 us (9%)
  matrix products  19.9 us (9%)
  other arithmetic  17.8 us (8%)
  between operations  15.3 us (7%)
  local copies, waits for them, and re-layouts  3.33 us (1%)
    ppermute x6, waiting for transfers between devices, swap(): return lax.ppermute(value, axis, [(0, 1), (1, 0)])  42.7 us
    all_gather x1, blocking collectives, on_device(): every = lax.all_gather(stats, BATCH)  42.2 us
    ppermute x8, waiting for transfers between devices, butterfly(): lax.ppermute(value, axis, [(i, i ^ step) for i in range(size)])  34.7 us
    ppermute x2, waiting for transfers between devices, transpose_blocks(): return lax.ppermute(value, PLANE, pairs)  15.2 us
    all_gather x1, waiting for transfers between devices, on_device(): slope = lax.all_gather(slope_pair, 'z', axis=0, tiled=True)  13.6 us
    ppermute x2, starting transfers between devices, transpose_blocks(): return lax.ppermute(value, PLANE, pairs)  9.94 us
    dot_general x1, matrix products, on_device(): lax.dot_general(norm_b, slope, (((1,), (1,)), ((), ())), preferred_elemen...  7.48 us
    ppermute x8, starting transfers between devices, butterfly(): lax.ppermute(value, axis, [(i, i ^ step) for i in range(size)])  6.29 us
  transfers between devices with their start and end apart: 20, of which 16 were waited for; matrix products, arithmetic and copies ran while one was open for 8% of the time, Pallas kernels for 0%

profile of v1, /device:TPU:4, one launch (start us, length us, event | category | flops | bytes accessed | tf_op | source)
XLA Modules:
  0.0 225.1 jit_solution(12757058952746672889)
XLA Ops:
  7.2 5.0 %collective-permute-start = (bf16[256,1024]{1,0:T(8,128)(2,1)}, bf16[256,1024]{1,0:T(8,128)(2,1)S(1)}, u32[]{:S(2)}, u32[]{:S(2)}) collective-permute-start(bf16[256,1024]{1,0:T(8,128)(2,1)} %param.3), channel_id=1, source_target_pairs={{0,0},{1,64},{2,128},{3,192},{64,1},{65,65},{66,129},{67,193},{128... | collective-permute-start | bytes 1572872 | tf_op jit(solution)/shard_map/gather/ppermute | solution.py:30
  12.3 15.2 %collective-permute-done = bf16[256,1024]{1,0:T(8,128)(2,1)S(1)} collective-permute-done((bf16[256,1024]{1,0:T(8,128)(2,1)}, bf16[256,1024]{1,0:T(8,128)(2,1)S(1)}, u32[]{:S(2)}, u32[]{:S(2)}) %collective-permute-start) | collective-permute-done | bytes 524320 | tf_op jit(solution)/shard_map/gather/ppermute | solution.py:30
  27.6 14.7 %collective-permute-done.1 = bf16[256,1024]{1,0:T(8,128)(2,1)S(1)} collective-permute-done((bf16[256,1024]{1,0:T(8,128)(2,1)S(1)}, bf16[256,1024]{1,0:T(8,128)(2,1)S(1)}, u32[]{:S(2)}, u32[]{:S(2)}) %collective-permute-start.1) | collective-permute-done | bytes 524320 | tf_op jit(solution)/shard_map/gather/ppermute | solution.py:16
  42.5 2.6 %collective-permute-done.2 = bf16[512,1024]{1,0:T(8,128)(2,1)S(1)} collective-permute-done((bf16[512,1024]{1,0:T(8,128)(2,1)S(1)}, bf16[512,1024]{1,0:T(8,128)(2,1)S(1)}, u32[]{:S(2)}, u32[]{:S(2)}) %collective-permute-start.2) | collective-permute-done | bytes 1048608 | tf_op jit(solution)/shard_map/gather/ppermute | solution.py:16
  47.1 2.1 convert_reduce_fusion
  49.4 5.0 %fusion.30 = bf16[1024,1024]{1,0:T(8,128)(2,1)} fusion(f32[1024]{0:T(1024)S(1)} %broadcast_multiply_fusion.3, bf16[1024,1024]{1,0:T(8,128)(2,1)S(1)} %copy-done, f32[1024]{0:T(1024)S(1)} %broadcast_multiply_fusion.4, bf16[256,1024]{1,0:T(8,128)(2,1)} %copy-done.1, bf16[256,1024]{1,0:T(8,128)(2,1)S(1)} %get-tuple-element.26, ...), kind=kOutput, calls=%fused_computation.44 | convolution fusion | flops 2162163712 | bytes 6299648 | tf_op jit(solution)/shard_map/corr/dot_general | solution.py:72
  54.9 2.5 %fusion.13 = (f32[1024]{0:T(1024)S(1)}, f32[1024]{0:T(1024)S(1)}, f32[1024]{0:T(1024)S(1)}) fusion(bf16[1024,1024]{1,0:T(8,128)(2,1)S(1)} %copy-done, f32[1024]{0:T(1024)S(1)} %broadcast_multiply_fusion.3, f32[1024]{0:T(1024)S(1)} %broadcast_multiply_fusion.4, bf16[256,1024]{1,0:T(8,128)(2,1)} %copy-done.1, bf16[256,1024]{1,0:T(8,128)(2,1)S(1)} %get-tuple-element.26, ...), kind=kLoop, calls=%fused_computation.26 | loop fusion | flops 17822720 | bytes 4214784 | tf_op jit(solution)/shard_map/local_stats/reduce_sum | solution.py:67
  57.4 42.2 %all-gather.1 = f32[16,5,1024]{2,1,0:T(8,128)S(1)} all-gather(f32[1,5,1024]{2,1,0:T(8,128)S(1)} %bitcast.55), channel_id=2, replica_groups=mesh['y'=4,'xl'=2,'z'=8,'xh'=2,'co'=2] {'xl','z'}, dimensions={0}, use_global_device_ids=true | all-gather | bytes 348160 | tf_op jit(solution)/shard_map/global_stats/all_gather | solution.py:85
  104.3 4.5 %collective-permute-done.3 = bf16[64,1024]{1,0:T(8,128)(2,1)S(1)} collective-permute-done((bf16[64,1024]{1,0:T(8,128)(2,1)S(1)}, bf16[64,1024]{1,0:T(8,128)(2,1)S(1)}, u32[]{:S(2)}, u32[]{:S(2)}) %collective-permute-start.3) | collective-permute-done | bytes 131104 | tf_op jit(solution)/shard_map/corr/ppermute | solution.py:16
  111.3 4.0 %collective-permute-done.4 = bf16[64,1024]{1,0:T(8,128)(2,1)S(1)} collective-permute-done((bf16[64,1024]{1,0:T(8,128)(2,1)S(1)}, bf16[64,1024]{1,0:T(8,128)(2,1)S(1)}, u32[]{:S(2)}, u32[]{:S(2)}) %collective-permute-start.4) | collective-permute-done | bytes 131104 | tf_op jit(solution)/shard_map/slope/ppermute | solution.py:16
  121.0 2.6 %collective-permute-done.5 = f32[3,1024]{1,0:T(4,128)S(1)} collective-permute-done((f32[3,1024]{1,0:T(4,128)S(1)}, f32[3,1024]{1,0:T(4,128)S(1)}, u32[]{:S(2)}, u32[]{:S(2)}) %collective-permute-start.5) | collective-permute-done | bytes 12320 | tf_op jit(solution)/shard_map/small_sums/ppermute | solution.py:23
  123.7 3.9 %collective-permute-done.6 = f32[3,1024]{1,0:T(4,128)S(1)} collective-permute-done((f32[3,1024]{1,0:T(4,128)S(1)}, f32[3,1024]{1,0:T(4,128)S(1)}, u32[]{:S(2)}, u32[]{:S(2)}) %collective-permute-start.6) | collective-permute-done | bytes 12320 | tf_op jit(solution)/shard_map/small_sums/ppermute | solution.py:23
  127.7 4.6 %collective-permute-done.7 = f32[3,1024]{1,0:T(4,128)S(1)} collective-permute-done((f32[3,1024]{1,0:T(4,128)S(1)}, f32[3,1024]{1,0:T(4,128)S(1)}, u32[]{:S(2)}, u32[]{:S(2)}) %collective-permute-start.7) | collective-permute-done | bytes 12320 | tf_op jit(solution)/shard_map/small_sums/ppermute | solution.py:23
  133.1 7.1 %collective-permute-done.8 = f32[3,1024]{1,0:T(4,128)S(1)} collective-permute-done((f32[3,1024]{1,0:T(4,128)S(1)}, f32[3,1024]{1,0:T(4,128)S(1)}, u32[]{:S(2)}, u32[]{:S(2)}) %collective-permute-start.8) | collective-permute-done | bytes 12320 | tf_op jit(solution)/shard_map/small_sums/ppermute | solution.py:23
  140.2 13.6 %all-gather.7.cloned.1.call-done = bf16[1024,1024]{1,0:T(8,128)(2,1)} async-done(((bf16[128,1024]{1,0:T(8,128)(2,1)}), bf16[1024,1024]{1,0:T(8,128)(2,1)}) %all-gather.7.cloned.1.call-update) | async-done | bytes 2097168 | tf_op jit(solution)/shard_map/slope/all_gather | solution.py:139
  153.7 4.2 %fusion.21 = (f32[1024]{0:T(1024)S(1)}, f32[1024]{0:T(1024)S(1)}, f32[1024]{0:T(1024)S(1)}, f32[1024]{0:T(1024)S(1)}) fusion(bf16[1024,1024]{1,0:T(8,128)(2,1)} %all-gather.7.cloned.1.call-done, f32[1024]{0:T(1024)S(1)} %bitcast.65, pred[]{:T(512)S(6)} %eq.31, f32[1024]{0:T(1024)S(1)} %bitcast.64), kind=kLoop, calls=%fused_computation.34 | loop fusion | flops 12578816 | bytes 2121729 | tf_op jit(solution)/shard_map/back/reduce_sum | solution.py:162
  158.0 7.5 %fusion.7 = bf16[1024,1024]{1,0:T(8,128)(2,1)} fusion(f32[1024]{0:T(1024)S(1)} %get-tuple-element.43, f32[1024]{0:T(1024)S(1)} %get-tuple-element.9, f32[1024]{0:T(1024)S(1)} %copy-done.8, bf16[1024,1024]{1,0:T(8,128)(2,1)} %all-gather.7.cloned.1.call-done, f32[1024]{0:T(1024)S(1)} %broadcast_multiply_fusion.1, bf16[1024,1024]{1,0:T(8,128)(2,1)S(1)} %copy-done, ...), kind=kOutput, calls=%fused_computation.20 | convolution fusion | flops 2169503744 | bytes 8413184 | tf_op jit(solution)/shard_map/back/dot_general | solution.py:163
  165.5 5.9 %fusion.10 = bf16[1024,1024]{1,0:T(8,128)(2,1)S(1)} fusion(f32[1024]{0:T(1024)S(1)} %get-tuple-element.42, f32[1024]{0:T(1024)S(1)} %get-tuple-element.6, f32[1024]{0:T(1024)S(1)} %get-tuple-element.21, bf16[1024,1024]{1,0:T(8,128)(2,1)} %all-gather.7.cloned.1.call-done, bf16[1024,1024]{1,0:T(8,128)(2,1)S(1)} %copy-done, f32[1024]{0:T(1024)S(1)} %copy-done.8, ...), kind=kOutput, calls=%fused_computation.23 | convolution fusion | flops 2169503744 | bytes 8413184 | tf_op jit(solution)/shard_map/back/dot_general | solution.py:167
  171.6 2.6 %collective-permute-done.9 = bf16[2,256,1024]{2,1,0:T(8,128)(2,1)S(1)} collective-permute-done((bf16[2,256,1024]{2,1,0:T(8,128)(2,1)S(1)}, bf16[2,256,1024]{2,1,0:T(8,128)(2,1)S(1)}, u32[]{:S(2)}, u32[]{:S(2)}) %collective-permute-start.9) | collective-permute-done | bytes 1048608 | tf_op jit(solution)/shard_map/reduce/ppermute | solution.py:16
  176.3 14.2 %collective-permute-done.10 = bf16[256,1024]{1,0:T(8,128)(2,1)S(1)} collective-permute-done((bf16[256,1024]{1,0:T(8,128)(2,1)S(1)}, bf16[256,1024]{1,0:T(8,128)(2,1)S(1)}, u32[]{:S(2)}, u32[]{:S(2)}) %collective-permute-start.10) | collective-permute-done | bytes 524320 | tf_op jit(solution)/shard_map/reduce/ppermute | solution.py:16
  190.8 4.9 %collective-permute-start.11 = (bf16[256,1024]{1,0:T(8,128)(2,1)S(1)}, bf16[256,1024]{1,0:T(8,128)(2,1)S(1)}, u32[]{:S(2)}, u32[]{:S(2)}) collective-permute-start(bf16[256,1024]{1,0:T(8,128)(2,1)S(1)} %fusion.37), channel_id=1, source_target_pairs={{0,0},{1,64},{2,128},{3,192},{64,1},{65,65},{66,129},{67,193},{128... | collective-permute-start | bytes 1572872 | tf_op jit(solution)/shard_map/reduce/ppermute | solution.py:30
  196.9 10.3 %collective-permute-done.13 = f32[1,128]{1,0:T(1,128)S(1)} collective-permute-done((f32[1,128]{1,0:T(1,128)S(1)}, f32[1,128]{1,0:T(1,128)S(1)}, u32[]{:S(2)}, u32[]{:S(2)}) %collective-permute-start.13) | collective-permute-done | bytes 544 | tf_op jit(solution)/shard_map/small_sums/ppermute | solution.py:23
  207.2 3.5 %collective-permute-done.14 = f32[1,128]{1,0:T(1,128)S(1)} collective-permute-done((f32[1,128]{1,0:T(1,128)S(1)}, f32[1,128]{1,0:T(1,128)S(1)}, u32[]{:S(2)}, u32[]{:S(2)}) %collective-permute-start.14) | collective-permute-done | bytes 544 | tf_op jit(solution)/shard_map/small_sums/ppermute | solution.py:23
  210.7 4.3 %collective-permute-start.15 = (f32[1,128]{1,0:T(1,128)S(1)}, f32[1,128]{1,0:T(1,128)S(1)}, u32[]{:S(2)}, u32[]{:S(2)}) collective-permute-start(f32[1,128]{1,0:T(1,128)S(1)} %add.187), channel_id=1, source_target_pairs={{0,128},{64,192},{128,0},{192,64},{1,129},{65,193},{129,1},{193,65... | collective-permute-start | bytes 1544 | tf_op jit(solution)/shard_map/small_sums/ppermute | solution.py:23
  (91 shorter events, 22.7 us)
Async XLA Ops:
  7.2 40.0 %all-gather.5.cloned.1.call-start = ((), (), s32[]{:S(2)}) async-start(), calls=%async_computation.2 | async-start | bytes 2621440 | tf_op jit(solution)/shard_map/gather/all_gather | solution.py:43
  7.2 20.3 %collective-permute-start = (bf16[256,1024]{1,0:T(8,128)(2,1)}, bf16[256,1024]{1,0:T(8,128)(2,1)S(1)}, u32[]{:S(2)}, u32[]{:S(2)}) collective-permute-start(bf16[256,1024]{1,0:T(8,128)(2,1)} %param.3), channel_id=1, source_target_pairs={{0,0},{1,64},{2,128},{3,192},{64,1},{65,65},{66,129},{67,193},{128... | collective-permute-start | bytes 1572872 | tf_op jit(solution)/shard_map/gather/ppermute | solution.py:30
  12.3 89.7 %reduce-scatter.3.cloned.1.call-start = ((), (), s32[]{:S(2)}) async-start(), calls=%async_computation.3 | async-start | bytes 2359296 | tf_op jit(solution)/shard_map/corr/reduce_scatter | solution.py:78
  27.6 14.7 %collective-permute-start.1 = (bf16[256,1024]{1,0:T(8,128)(2,1)S(1)}, bf16[256,1024]{1,0:T(8,128)(2,1)S(1)}, u32[]{:S(2)}, u32[]{:S(2)}) collective-permute-start(bf16[256,1024]{1,0:T(8,128)(2,1)S(1)} %collective-permute-done), channel_id=1, source_target_pairs={{0,2},{2,0},{1,3},{3,1},{4,6},{6,4},{5,7},{7,5},{8,10},{10,8},{9,1... | collective-permute-start | bytes 1572872 | tf_op jit(solution)/shard_map/gather/ppermute | solution.py:16
  42.4 2.7 %collective-permute-start.2 = (bf16[512,1024]{1,0:T(8,128)(2,1)S(1)}, bf16[512,1024]{1,0:T(8,128)(2,1)S(1)}, u32[]{:S(2)}, u32[]{:S(2)}) collective-permute-start(bf16[512,1024]{1,0:T(8,128)(2,1)S(1)} %pad_maximum_fusion.1), channel_id=1, source_target_pairs={{0,1},{1,0},{2,3},{3,2},{4,5},{5,4},{6,7},{7,6},{8,9},{9,8},{10,11... | collective-permute-start | bytes 3145736 | tf_op jit(solution)/shard_map/gather/ppermute | solution.py:16
  47.1 2.2 copy-start
  54.3 99.4 %all-gather.7.cloned.1.call-start = ((), (), s32[]{:S(2)}) async-start(), calls=%async_computation.4 | async-start | bytes 2359296 | tf_op jit(solution)/shard_map/slope/all_gather | solution.py:139
  102.9 5.8 %collective-permute-start.3 = (bf16[64,1024]{1,0:T(8,128)(2,1)S(1)}, bf16[64,1024]{1,0:T(8,128)(2,1)S(1)}, u32[]{:S(2)}, u32[]{:S(2)}) collective-permute-start(bf16[64,1024]{1,0:T(8,128)(2,1)S(1)} %broadcast_select_fusion.6), channel_id=1, source_target_pairs={{0,32},{32,0},{1,33},{33,1},{2,34},{34,2},{3,35},{35,3},{4,36},{36... | collective-permute-start | bytes 393224 | tf_op jit(solution)/shard_map/corr/ppermute | solution.py:16
  110.3 5.1 %collective-permute-start.4 = (bf16[64,1024]{1,0:T(8,128)(2,1)S(1)}, bf16[64,1024]{1,0:T(8,128)(2,1)S(1)}, u32[]{:S(2)}, u32[]{:S(2)}) collective-permute-start(bf16[64,1024]{1,0:T(8,128)(2,1)S(1)} %get-tuple-element.44), channel_id=1, source_target_pairs={{0,32},{32,0},{1,33},{33,1},{2,34},{34,2},{3,35},{35,3},{4,36},{36... | collective-permute-start | bytes 393224 | tf_op jit(solution)/shard_map/slope/ppermute | solution.py:16
  116.2 100.4 %reduce-scatter.5.cloned.1.call-start = ((), (), s32[]{:S(2)}) async-start(), calls=%async_computation.5 | async-start | bytes 2621440 | tf_op jit(solution)/shard_map/reduce/reduce_scatter | solution.py:171
  117.6 40.4 %copy-start.8 = (f32[1024]{0:T(1024)S(1)}, f32[1024]{0:T(1024)}, u32[]{:S(2)}) copy-start(f32[1024]{0:T(1024)} %copy-done.7) | copy-start | bytes 12292
  119.8 3.8 %collective-permute-start.5 = (f32[3,1024]{1,0:T(4,128)S(1)}, f32[3,1024]{1,0:T(4,128)S(1)}, u32[]{:S(2)}, u32[]{:S(2)}) collective-permute-start(f32[3,1024]{1,0:T(4,128)S(1)} %maximum_maximum_fusion), channel_id=1, source_target_pairs={{0,32},{32,0},{1,33},{33,1},{2,34},{34,2},{3,35},{35,3},{4,36},{36... | collective-permute-start | bytes 36872 | tf_op jit(solution)/shard_map/small_sums/ppermute | solution.py:23
  123.7 3.9 %collective-permute-start.6 = (f32[3,1024]{1,0:T(4,128)S(1)}, f32[3,1024]{1,0:T(4,128)S(1)}, u32[]{:S(2)}, u32[]{:S(2)}) collective-permute-start(f32[3,1024]{1,0:T(4,128)S(1)} %fusion.50), channel_id=1, source_target_pairs={{0,4},{4,0},{8,12},{12,8},{16,20},{20,16},{24,28},{28,24},{1,5},{5... | collective-permute-start | bytes 36872 | tf_op jit(solution)/shard_map/small_sums/ppermute | solution.py:23
  127.7 4.7 %collective-permute-start.7 = (f32[3,1024]{1,0:T(4,128)S(1)}, f32[3,1024]{1,0:T(4,128)S(1)}, u32[]{:S(2)}, u32[]{:S(2)}) collective-permute-start(f32[3,1024]{1,0:T(4,128)S(1)} %fusion.56), channel_id=1, source_target_pairs={{0,8},{4,12},{8,0},{12,4},{16,24},{20,28},{24,16},{28,20},{1,9},{5... | collective-permute-start | bytes 36872 | tf_op jit(solution)/shard_map/small_sums/ppermute | solution.py:23
  132.4 7.8 %collective-permute-start.8 = (f32[3,1024]{1,0:T(4,128)S(1)}, f32[3,1024]{1,0:T(4,128)S(1)}, u32[]{:S(2)}, u32[]{:S(2)}) collective-permute-start(f32[3,1024]{1,0:T(4,128)S(1)} %add.179), channel_id=1, source_target_pairs={{0,16},{4,20},{8,24},{12,28},{16,0},{20,4},{24,8},{28,12},{1,17},{... | collective-permute-start | bytes 36872 | tf_op jit(solution)/shard_map/small_sums/ppermute | solution.py:23
  153.7 4.3 %copy-start.3 = (bf16[256,1024]{1,0:T(8,128)(2,1)S(1)}, bf16[256,1024]{1,0:T(8,128)(2,1)}, u32[]{:S(2)}) copy-start(bf16[256,1024]{1,0:T(8,128)(2,1)} %copy-done.1) | copy-start | bytes 1572868
  153.7 4.3 %copy-start.6 = (bf16[256,1024]{1,0:T(8,128)(2,1)S(1)}, bf16[256,1024]{1,0:T(8,128)(2,1)}, u32[]{:S(2)}) copy-start(bf16[256,1024]{1,0:T(8,128)(2,1)} %copy-done.4) | copy-start | bytes 1572868
  171.5 2.7 %collective-permute-start.9 = (bf16[2,256,1024]{2,1,0:T(8,128)(2,1)S(1)}, bf16[2,256,1024]{2,1,0:T(8,128)(2,1)S(1)}, u32[]{:S(2)}, u32[]{:S(2)}) collective-permute-start(bf16[2,256,1024]{2,1,0:T(8,128)(2,1)S(1)} %select_bitcast_fusion), channel_id=1, source_target_pairs={{0,1},{1,0},{2,3},{3,2},{4,5},{5,4},{6,7},{7,6},{8,9},{9,8},{10,11... | collective-permute-start | bytes 3145736 | tf_op jit(solution)/shard_map/reduce/ppermute | solution.py:16
  174.9 15.6 %collective-permute-start.10 = (bf16[256,1024]{1,0:T(8,128)(2,1)S(1)}, bf16[256,1024]{1,0:T(8,128)(2,1)S(1)}, u32[]{:S(2)}, u32[]{:S(2)}) collective-permute-start(bf16[256,1024]{1,0:T(8,128)(2,1)S(1)} %fusion.38), channel_id=1, source_target_pairs={{0,2},{2,0},{1,3},{3,1},{4,6},{6,4},{5,7},{7,5},{8,10},{10,8},{9,1... | collective-permute-start | bytes 1572872 | tf_op jit(solution)/shard_map/reduce/ppermute | solution.py:16
  190.8 25.8 %collective-permute-start.11 = (bf16[256,1024]{1,0:T(8,128)(2,1)S(1)}, bf16[256,1024]{1,0:T(8,128)(2,1)S(1)}, u32[]{:S(2)}, u32[]{:S(2)}) collective-permute-start(bf16[256,1024]{1,0:T(8,128)(2,1)S(1)} %fusion.37), channel_id=1, source_target_pairs={{0,0},{1,64},{2,128},{3,192},{64,1},{65,65},{66,129},{67,193},{128... | collective-permute-start | bytes 1572872 | tf_op jit(solution)/shard_map/reduce/ppermute | solution.py:30
  195.7 1.2 collective-permute-start.12
  196.9 10.3 %collective-permute-start.13 = (f32[1,128]{1,0:T(1,128)S(1)}, f32[1,128]{1,0:T(1,128)S(1)}, u32[]{:S(2)}, u32[]{:S(2)}) collective-permute-start(f32[1,128]{1,0:T(1,128)S(1)} %slice_add_fusion), channel_id=1, source_target_pairs={{0,2},{2,0},{1,3},{3,1},{4,6},{6,4},{5,7},{7,5},{8,10},{10,8},{9,1... | collective-permute-start | bytes 1544 | tf_op jit(solution)/shard_map/small_sums/ppermute | solution.py:23
  207.2 3.5 %collective-permute-start.14 = (f32[1,128]{1,0:T(1,128)S(1)}, f32[1,128]{1,0:T(1,128)S(1)}, u32[]{:S(2)}, u32[]{:S(2)}) collective-permute-start(f32[1,128]{1,0:T(1,128)S(1)} %add.186), channel_id=1, source_target_pairs={{0,64},{64,0},{128,192},{192,128},{1,65},{65,1},{129,193},{193,129... | collective-permute-start | bytes 1544 | tf_op jit(solution)/shard_map/small_sums/ppermute | solution.py:23
  210.7 5.8 %collective-permute-start.15 = (f32[1,128]{1,0:T(1,128)S(1)}, f32[1,128]{1,0:T(1,128)S(1)}, u32[]{:S(2)}, u32[]{:S(2)}) collective-permute-start(f32[1,128]{1,0:T(1,128)S(1)} %add.187), channel_id=1, source_target_pairs={{0,128},{64,192},{128,0},{192,64},{1,129},{65,193},{129,1},{193,65... | collective-permute-start | bytes 1544 | tf_op jit(solution)/shard_map/small_sums/ppermute | solution.py:23
  (7 other events, 10.2 us)
Sparse Core Ops, SparseCore 0:
  12.4 34.3 all-gather.4
  54.5 46.2 reduce-scatter.2
  116.3 37.4 all-gather.6
  165.6 30.9 reduce-scatter.4

commit v2 on v1

--- a/solution.py
+++ b/solution.py
@@ -49,7 +49,9 @@
         other = swap(pair, "co")
         even = jnp.where(co == 0, pair, other)
         odd = jnp.where(co == 0, other, pair)
-        block_b = jnp.concatenate([even[:rows], odd[:rows], even[rows:], odd[rows:]], 0)
+        block_b = lax.optimization_barrier(
+            jnp.concatenate([even[:rows], odd[:rows], even[rows:], odd[rows:]], 0)
+        )
 
     with jax.named_scope("local_stats"):
         value_a = block_a.astype(f32)
@@ -76,13 +78,12 @@
             preferred_element_type=f32,
         ).astype(bf16)
         summed = lax.psum_scatter(product, "z", scatter_dimension=0, tiled=True)
-        half = summed.shape[0] // 2
-        low, high = summed[:half], summed[half:]
-        received = swap(jnp.where(xl == 0, high, low), "xl")
-        piece = jnp.where(xl == 0, low, high).astype(f32) + received.astype(f32)
+        piece = summed.astype(f32) + swap(summed, "xl").astype(f32)
 
     with jax.named_scope("global_stats"):
-        every = lax.all_gather(stats, BATCH)
+        every = lax.all_to_all(
+            jnp.broadcast_to(stats, (parts,) + stats.shape), BATCH, 0, 0, tiled=True
+        )
         mean_a = jnp.sum(every[:, 0], 0) / parts
         mean_b = jnp.sum(every[:, 2], 0) / parts
         shift_a = every[:, 0] - mean_a
@@ -99,17 +100,22 @@
         )
 
     with jax.named_scope("norm"):
-        norm_a = ((value_a - mean_a) * scale_a).astype(bf16)
-        norm_b = ((value_b - mean_b) * scale_b).astype(bf16)
+        norm_a, norm_b = lax.optimization_barrier(
+            (
+                ((value_a - mean_a) * scale_a).astype(bf16),
+                ((value_b - mean_b) * scale_b).astype(bf16),
+            )
+        )
         plain_a = norm_a.astype(f32)
         plain_b = norm_b.astype(f32)
         norm_sums = jnp.stack([jnp.sum(plain_a, 0), jnp.sum(plain_b, 0)])
 
     with jax.named_scope("slope"):
         diagonal_block = y == xh * 2 + co
-        first_row = z * (2 * half) + xl * half
-        row_shift = lax.dynamic_slice_in_dim(shift_a, first_row, half, 1)
-        row_scale = lax.dynamic_slice_in_dim(scale_a, first_row, half, 0)
+        height = piece.shape[0]
+        first_row = z * height
+        row_shift = lax.dynamic_slice_in_dim(shift_a, first_row, height, 1)
+        row_scale = lax.dynamic_slice_in_dim(scale_a, first_row, height, 0)
         between = lax.dot_general(
             row_shift,
             shift_b,
@@ -125,47 +131,47 @@
         slope_piece = jnp.where(
             diagonal, diag_slope[None, :], (2.0 * off_weight * corr).astype(bf16)
         )
-        loss_piece = jnp.sum(
-            jnp.where(diagonal, (1.0 - diag_corr) ** 2, off_weight * corr * corr)
+        slope = lax.all_gather(slope_piece, "z", axis=0, tiled=True)
+
+    with jax.named_scope("small_sums"):
+        exact = jnp.where(diagonal, diag_corr[None, :], corr)
+        weighed = 0.5 * (slope_piece.astype(f32) * exact)
+        loss_piece = 0.5 * jnp.sum(
+            jnp.where(diagonal, (1.0 - exact) ** 2, off_weight * exact * exact)
         )
-        slope_other = swap(slope_piece, "xl")
-        slope_pair = jnp.concatenate(
+        placed = lax.dynamic_update_slice_in_dim(
+            jnp.zeros((width,), f32), jnp.sum(weighed, 1), first_row, 0
+        )
+        small = jnp.concatenate(
             [
-                jnp.where(xl == 0, slope_piece, slope_other),
-                jnp.where(xl == 0, slope_other, slope_piece),
+                norm_sums,
+                placed[None],
+                jnp.sum(weighed, 0)[None],
+                jnp.full((1, width), loss_piece),
             ],
             0,
         )
-        slope = lax.all_gather(slope_pair, "z", axis=0, tiled=True)
-
-    with jax.named_scope("small_sums"):
-        small = jnp.concatenate([norm_sums, jnp.full((1, width), loss_piece)], 0)
         small = butterfly(butterfly(small, "xl"), "z")
-        loss_total = small[2:3, :128]
+        loss_total = small[4:5, :128]
         loss_total = butterfly(butterfly(butterfly(loss_total, "co"), "xh"), "y")
+        slope, small, loss_total = lax.optimization_barrier((slope, small, loss_total))
         loss_mean = loss_total[0, 0] / full_width
-        centre_a = small[0:1] / total
-        centre_b = small[1:2] / total
+        centre_a = small[0] / total
+        centre_b = small[1] / total
+        two_a = small[2]
+        two_b = small[3]
 
     with jax.named_scope("back"):
         wide = slope.astype(f32)
-        eye = jnp.logical_and(
-            lax.broadcasted_iota(jnp.int32, slope.shape, 0)
-            == lax.broadcasted_iota(jnp.int32, slope.shape, 1),
-            diagonal_block,
-        )
-        squares = jnp.where(eye, 0.0, wide * wide) / (2.0 * off_weight)
-        diag_term = jnp.where(diagonal_block, diag_slope.astype(f32) * diag_corr, 0.0)
-        two_a = jnp.sum(squares, 1) + diag_term
-        two_b = jnp.sum(squares, 0) + diag_term
         one_a = jnp.sum(wide * centre_b, 1)
         one_b = jnp.sum(wide * centre_a.reshape(width, 1), 0)
+        back_b = jnp.dot(norm_a, slope, preferred_element_type=f32)
+        part_b = ((back_b - one_b - plain_b * two_b) * scale_b).astype(bf16)
+        part_b, norm_b, slope = lax.optimization_barrier((part_b, norm_b, slope))
         back_a = lax.dot_general(
             norm_b, slope, (((1,), (1,)), ((), ())), preferred_element_type=f32
         )
         part_a = ((back_a - one_a - plain_a * two_a) * scale_a).astype(bf16)
-        back_b = jnp.dot(norm_a, slope, preferred_element_type=f32)
-        part_b = ((back_b - one_b - plain_b * two_b) * scale_b).astype(bf16)
 
     with jax.named_scope("reduce"):
         grad_a = lax.psum_scatter(part_a, "y", scatter_dimension=0, tiled=True)

time: 228 us -> 239 us (1.048)
  waiting for transfers between devices: 106 us -> 157 us
  blocking collectives: 42.2 us -> 0 us
  starting transfers between devices: 20.3 us -> 29.6 us
  other arithmetic: 17.8 us -> 13.4 us
  matrix products: 19.9 us -> 16.3 us
    all_gather x1 -> x0, blocking collectives: 42.2 us -> none  [on_device(): every = lax.all_gather(stats, BATCH)]
    all_to_all x0 -> x1, waiting for transfers between devices: none -> 22.6 us  [on_device(): lax.all_to_all(jnp.broadcast_to(stats, (parts,) + stats.shape), BATCH, 0,...]
    all_gather x1, waiting for transfers between devices: 0.02 us -> 18.5 us  [on_device(): block_a = lax.all_gather(embed_a, 'y', axis=0, tiled=True)]
    reduce_scatter x1, waiting for transfers between devices: 0.01 us -> 17.4 us  [on_device(): summed = lax.psum_scatter(product, 'z', scatter_dimension=0, tiled=True)]
    ppermute x2, waiting for transfers between devices: 15.2 us -> 31.9 us  [transpose_blocks(): return lax.ppermute(value, PLANE, pairs)]
    all_gather x1, waiting for transfers between devices: 13.6 us -> 0.01 us  [on_device(): slope = lax.all_gather(slope_piece, 'z', axis=0, tiled=True)]
    ppermute x8, waiting for transfers between devices: 34.7 us -> 25.8 us  [butterfly(): lax.ppermute(value, axis, [(i, i ^ step) for i in range(size)])]
    all_to_all x0 -> x1, starting transfers between devices: none -> 7.73 us  [on_device(): lax.all_to_all(jnp.broadcast_to(stats, (parts,) + stats.shape), BATCH, 0,...]
  transfers between devices with their start and end apart: 20 -> 20, of which waited for: 16 -> 18; matrix products, arithmetic and copies ran while one was open for 8% -> 4% of each run, Pallas kernels for 0% -> 0%
where the time goes in v2:
time: 239 us; the launch traced here: 237 us
  waiting for transfers between devices  157 us (66%)
  starting transfers between devices  29.6 us (12%)
  matrix products  16.3 us (7%)
  between operations  15.9 us (7%)
  other arithmetic  13.4 us (6%)
  local copies, waits for them, and re-layouts  5.35 us (2%)
    ppermute x5, waiting for transfers between devices, swap(): return lax.ppermute(value, axis, [(0, 1), (1, 0)])  40.6 us
    ppermute x2, waiting for transfers between devices, transpose_blocks(): return lax.ppermute(value, PLANE, pairs)  31.9 us
    ppermute x8, waiting for transfers between devices, butterfly(): lax.ppermute(value, axis, [(i, i ^ step) for i in range(size)])  25.8 us
    all_to_all x1, waiting for transfers between devices, on_device(): lax.all_to_all(jnp.broadcast_to(stats, (parts,) + stats.shape), BATCH, 0,...  22.6 us
    all_gather x1, waiting for transfers between devices, on_device(): block_a = lax.all_gather(embed_a, 'y', axis=0, tiled=True)  18.5 us
    reduce_scatter x1, waiting for transfers between devices, on_device(): summed = lax.psum_scatter(product, 'z', scatter_dimension=0, tiled=True)  17.4 us
    ppermute x8, starting transfers between devices, butterfly(): lax.ppermute(value, axis, [(i, i ^ step) for i in range(size)])  11.7 us
    ppermute x2, starting transfers between devices, transpose_blocks(): return lax.ppermute(value, PLANE, pairs)  8.47 us
  transfers between devices with their start and end apart: 20, of which 18 were waited for; matrix products, arithmetic and copies ran while one was open for 4% of the time, Pallas kernels for 0%

profile of v2, /device:TPU:4, one launch (start us, length us, event | category | flops | bytes accessed | tf_op | source)
XLA Modules:
  0.0 237.2 jit_solution(3135163274087000391)
XLA Ops:
  7.2 5.0 %collective-permute-start = (bf16[256,1024]{1,0:T(8,128)(2,1)}, bf16[256,1024]{1,0:T(8,128)(2,1)S(1)}, u32[]{:S(2)}, u32[]{:S(2)}) collective-permute-start(bf16[256,1024]{1,0:T(8,128)(2,1)} %param.3), channel_id=1, source_target_pairs={{0,0},{1,64},{2,128},{3,192},{64,1},{65,65},{66,129},{67,193},{128... | collective-permute-start | bytes 1572872 | tf_op jit(solution)/shard_map/gather/ppermute | solution.py:30
  12.3 15.3 %collective-permute-done = bf16[256,1024]{1,0:T(8,128)(2,1)S(1)} collective-permute-done((bf16[256,1024]{1,0:T(8,128)(2,1)}, bf16[256,1024]{1,0:T(8,128)(2,1)S(1)}, u32[]{:S(2)}, u32[]{:S(2)}) %collective-permute-start) | collective-permute-done | bytes 524320 | tf_op jit(solution)/shard_map/gather/ppermute | solution.py:30
  27.6 14.6 %collective-permute-done.1 = bf16[256,1024]{1,0:T(8,128)(2,1)S(1)} collective-permute-done((bf16[256,1024]{1,0:T(8,128)(2,1)S(1)}, bf16[256,1024]{1,0:T(8,128)(2,1)S(1)}, u32[]{:S(2)}, u32[]{:S(2)}) %collective-permute-start.1) | collective-permute-done | bytes 524320 | tf_op jit(solution)/shard_map/gather/ppermute | solution.py:16
  46.4 18.5 %all-gather.3.cloned.1.call-done = bf16[1024,1024]{1,0:T(8,128)(2,1)} async-done(((bf16[256,1024]{1,0:T(8,128)(2,1)}), bf16[1024,1024]{1,0:T(8,128)(2,1)}) %all-gather.3.cloned.1.call-update) | async-done | bytes 2097168 | tf_op jit(solution)/shard_map/gather/all_gather | solution.py:43
  67.1 3.8 %fusion.25 = bf16[1024,1024]{1,0:T(8,128)(2,1)} fusion(bf16[1024,1024]{1,0:T(8,128)(2,1)S(1)} %pad_maximum_fusion, f32[1024]{0:T(1024)S(1)} %broadcast_multiply_fusion.3, bf16[1024,1024]{1,0:T(8,128)(2,1)S(1)} %copy-done, f32[1024]{0:T(1024)S(1)} %broadcast_multiply_fusion.4), kind=kOutput, calls=%fused_computation.37 | convolution fusion | flops 2154823680 | bytes 6299648 | tf_op jit(solution)/shard_map/corr/dot_general | solution.py:74
  70.9 3.0 %fusion.15 = (f32[1024]{0:T(1024)S(1)}, f32[1024]{0:T(1024)S(1)}, f32[1024]{0:T(1024)S(1)}) fusion(bf16[1024,1024]{1,0:T(8,128)(2,1)S(1)} %pad_maximum_fusion, bf16[1024,1024]{1,0:T(8,128)(2,1)} %all-gather.3.cloned.1.call-done, f32[1024]{0:T(1024)S(1)} %broadcast_multiply_fusion.3, f32[1024]{0:T(1024)S(1)} %broadcast_multiply_fusion.4), kind=kLoop, calls=%fused_computation.27 | loop fusion | flops 10482688 | bytes 4214784 | tf_op jit(solution)/shard_map/local_stats/reduce_sum | solution.py:69
  74.8 7.7 %all-to-all-start = ((f32[16,5,1024]{2,1,0:T(8,128)}), f32[16,5,1024]{2,1,0:T(8,128)S(1)}, u32[]{:S(2)}, u32[]{:S(2)}) async-start(f32[16,5,1024]{2,1,0:T(8,128)} %broadcast_in_dim.26), calls=%async_computation | async-start | bytes 1048576 | tf_op jit(solution)/shard_map/global_stats/all_to_all | solution.py:84
  82.6 22.6 %all-to-all-done = f32[16,5,1024]{2,1,0:T(8,128)S(1)} async-done(((f32[16,5,1024]{2,1,0:T(8,128)}), f32[16,5,1024]{2,1,0:T(8,128)S(1)}, u32[]{:S(2)}, u32[]{:S(2)}) %all-to-all-start) | async-done | bytes 327712 | tf_op jit(solution)/shard_map/global_stats/all_to_all | solution.py:84
  105.6 17.4 %reduce-scatter.3.cloned.1.call-done = bf16[128,1024]{1,0:T(8,128)(2,1)} async-done(((bf16[1024,1024]{1,0:T(8,128)(2,1)}), bf16[128,1024]{1,0:T(8,128)(2,1)}) %reduce-scatter.3.cloned.1.call-update) | async-done | bytes 262160 | tf_op jit(solution)/shard_map/corr/reduce_scatter | solution.py:80
  123.9 5.6 %collective-permute-done.3 = bf16[128,1024]{1,0:T(8,128)(2,1)S(1)} collective-permute-done((bf16[128,1024]{1,0:T(8,128)(2,1)}, bf16[128,1024]{1,0:T(8,128)(2,1)S(1)}, u32[]{:S(2)}, u32[]{:S(2)}) %collective-permute-start.3) | collective-permute-done | bytes 262176 | tf_op jit(solution)/shard_map/corr/ppermute | solution.py:16
  138.6 3.0 %collective-permute-done.4 = f32[5,1024]{1,0:T(8,128)S(1)} collective-permute-done((f32[5,1024]{1,0:T(8,128)S(1)}, f32[5,1024]{1,0:T(8,128)S(1)}, u32[]{:S(2)}, u32[]{:S(2)}) %collective-permute-start.4) | collective-permute-done | bytes 20512 | tf_op jit(solution)/shard_map/small_sums/ppermute | solution.py:23
  142.0 3.9 %collective-permute-done.5 = f32[5,1024]{1,0:T(8,128)S(1)} collective-permute-done((f32[5,1024]{1,0:T(8,128)S(1)}, f32[5,1024]{1,0:T(8,128)S(1)}, u32[]{:S(2)}, u32[]{:S(2)}) %collective-permute-start.5) | collective-permute-done | bytes 20512 | tf_op jit(solution)/shard_map/small_sums/ppermute | solution.py:23
  145.9 2.8 %collective-permute-start.6 = (f32[5,1024]{1,0:T(8,128)S(1)}, f32[5,1024]{1,0:T(8,128)S(1)}, u32[]{:S(2)}, u32[]{:S(2)}) collective-permute-start(f32[5,1024]{1,0:T(8,128)S(1)} %add.140), channel_id=1, source_target_pairs={{0,8},{4,12},{8,0},{12,4},{16,24},{20,28},{24,16},{28,20},{1,9},{5... | collective-permute-start | bytes 61448 | tf_op jit(solution)/shard_map/small_sums/ppermute | solution.py:23
  148.7 3.1 %collective-permute-done.6 = f32[5,1024]{1,0:T(8,128)S(1)} collective-permute-done((f32[5,1024]{1,0:T(8,128)S(1)}, f32[5,1024]{1,0:T(8,128)S(1)}, u32[]{:S(2)}, u32[]{:S(2)}) %collective-permute-start.6) | collective-permute-done | bytes 20512 | tf_op jit(solution)/shard_map/small_sums/ppermute | solution.py:23
  151.8 4.5 %collective-permute-start.7 = (f32[5,1024]{1,0:T(8,128)S(1)}, f32[5,1024]{1,0:T(8,128)S(1)}, u32[]{:S(2)}, u32[]{:S(2)}) collective-permute-start(f32[5,1024]{1,0:T(8,128)S(1)} %add.141), channel_id=1, source_target_pairs={{0,16},{4,20},{8,24},{12,28},{16,0},{20,4},{24,8},{28,12},{1,17},{... | collective-permute-start | bytes 61448 | tf_op jit(solution)/shard_map/small_sums/ppermute | solution.py:23
  156.3 3.9 %collective-permute-done.7 = f32[5,1024]{1,0:T(8,128)S(1)} collective-permute-done((f32[5,1024]{1,0:T(8,128)S(1)}, f32[5,1024]{1,0:T(8,128)S(1)}, u32[]{:S(2)}, u32[]{:S(2)}) %collective-permute-start.7) | collective-permute-done | bytes 20512 | tf_op jit(solution)/shard_map/small_sums/ppermute | solution.py:23
  161.7 4.7 %collective-permute-done.9 = f32[1,128]{1,0:T(1,128)S(1)} collective-permute-done((f32[1,128]{1,0:T(1,128)S(1)}, f32[1,128]{1,0:T(1,128)S(1)}, u32[]{:S(2)}, u32[]{:S(2)}) %collective-permute-start.9) | collective-permute-done | bytes 544 | tf_op jit(solution)/shard_map/small_sums/ppermute | solution.py:23
  171.5 3.5 %collective-permute-done.11 = f32[1,128]{1,0:T(1,128)S(1)} collective-permute-done((f32[1,128]{1,0:T(1,128)S(1)}, f32[1,128]{1,0:T(1,128)S(1)}, u32[]{:S(2)}, u32[]{:S(2)}) %collective-permute-start.11) | collective-permute-done | bytes 544 | tf_op jit(solution)/shard_map/small_sums/ppermute | solution.py:23
  177.6 6.1 %fusion.10 = bf16[1024,1024]{1,0:T(8,128)(2,1)} fusion(bf16[1024,1024]{1,0:T(8,128)(2,1)S(1)} %copy-done.3, f32[1024]{0:T(1024)S(1)} %bitcast.71, f32[1024]{0:T(1024)S(1)} %get-tuple-element.22, f32[1024]{0:T(1024)S(1)} %get-tuple-element.37, bf16[1024,1024]{1,0:T(8,128)(2,1)} %copy-done.4, bf16[1024,1024]{1,0:T(8,128)(2,1)} %all-gather.5.cloned.1.call-done), kind=kOutput, calls=%fused_computation.22 | convolution fusion | flops 2153775104 | bytes 8400896 | tf_op jit(solution)/shard_map/back/dot_general | solution.py:168
  183.7 3.9 %fusion.7 = bf16[1024,1024]{1,0:T(8,128)(2,1)} fusion(bf16[1024,1024]{1,0:T(8,128)(2,1)S(1)} %copy-done.5, f32[1024]{0:T(1024)S(1)} %bitcast.70, f32[1024]{0:T(1024)S(1)} %get-tuple-element.23, f32[1024]{0:T(1024)S(1)} %get-tuple-element.38, bf16[1024,1024]{1,0:T(8,128)(2,1)S(1)} %copy-done.3, bf16[1024,1024]{1,0:T(8,128)(2,1)S(1)} %copy-done.7), kind=kOutput, calls=%fused_computation.19 | convolution fusion | flops 2153775104 | bytes 8400896 | tf_op jit(solution)/shard_map/back/dot_general | solution.py:171
  189.4 2.6 %collective-permute-done.12 = bf16[2,256,1024]{2,1,0:T(8,128)(2,1)S(1)} collective-permute-done((bf16[2,256,1024]{2,1,0:T(8,128)(2,1)S(1)}, bf16[2,256,1024]{2,1,0:T(8,128)(2,1)S(1)}, u32[]{:S(2)}, u32[]{:S(2)}) %collective-permute-start.12) | collective-permute-done | bytes 1048608 | tf_op jit(solution)/shard_map/reduce/ppermute | solution.py:16
  193.2 15.1 %collective-permute-done.13 = bf16[256,1024]{1,0:T(8,128)(2,1)S(1)} collective-permute-done((bf16[256,1024]{1,0:T(8,128)(2,1)S(1)}, bf16[256,1024]{1,0:T(8,128)(2,1)S(1)}, u32[]{:S(2)}, u32[]{:S(2)}) %collective-permute-start.13) | collective-permute-done | bytes 524320 | tf_op jit(solution)/shard_map/reduce/ppermute | solution.py:16
  208.6 3.4 %collective-permute-start.14 = (bf16[256,1024]{1,0:T(8,128)(2,1)S(1)}, bf16[256,1024]{1,0:T(8,128)(2,1)S(1)}, u32[]{:S(2)}, u32[]{:S(2)}) collective-permute-start(bf16[256,1024]{1,0:T(8,128)(2,1)S(1)} %fusion.30), channel_id=1, source_target_pairs={{0,0},{1,64},{2,128},{3,192},{64,1},{65,65},{66,129},{67,193},{128... | collective-permute-start | bytes 1572872 | tf_op jit(solution)/shard_map/reduce/ppermute | solution.py:30
  212.1 16.6 %collective-permute-done.14 = bf16[256,1024]{1,0:T(8,128)(2,1)S(1)} collective-permute-done((bf16[256,1024]{1,0:T(8,128)(2,1)S(1)}, bf16[256,1024]{1,0:T(8,128)(2,1)S(1)}, u32[]{:S(2)}, u32[]{:S(2)}) %collective-permute-start.14) | collective-permute-done | bytes 524320 | tf_op jit(solution)/shard_map/reduce/ppermute | solution.py:30
  (85 shorter events, 30.6 us)
Async XLA Ops:
  7.2 57.8 %all-gather.3.cloned.1.call-start = ((), (), s32[]{:S(2)}) async-start(), calls=%async_computation.3 | async-start | bytes 2621440 | tf_op jit(solution)/shard_map/gather/all_gather | solution.py:43
  7.2 20.3 %collective-permute-start = (bf16[256,1024]{1,0:T(8,128)(2,1)}, bf16[256,1024]{1,0:T(8,128)(2,1)S(1)}, u32[]{:S(2)}, u32[]{:S(2)}) collective-permute-start(bf16[256,1024]{1,0:T(8,128)(2,1)} %param.3), channel_id=1, source_target_pairs={{0,0},{1,64},{2,128},{3,192},{64,1},{65,65},{66,129},{67,193},{128... | collective-permute-start | bytes 1572872 | tf_op jit(solution)/shard_map/gather/ppermute | solution.py:30
  27.6 14.7 %collective-permute-start.1 = (bf16[256,1024]{1,0:T(8,128)(2,1)S(1)}, bf16[256,1024]{1,0:T(8,128)(2,1)S(1)}, u32[]{:S(2)}, u32[]{:S(2)}) collective-permute-start(bf16[256,1024]{1,0:T(8,128)(2,1)S(1)} %collective-permute-done), channel_id=1, source_target_pairs={{0,2},{2,0},{1,3},{3,1},{4,6},{6,4},{5,7},{7,5},{8,10},{10,8},{9,1... | collective-permute-start | bytes 1572872 | tf_op jit(solution)/shard_map/gather/ppermute | solution.py:16
  27.6 95.4 %reduce-scatter.3.cloned.1.call-start = ((), (), s32[]{:S(2)}) async-start(), calls=%async_computation.4 | async-start | bytes 2359296 | tf_op jit(solution)/shard_map/corr/reduce_scatter | solution.py:80
  42.4 2.7 %collective-permute-start.2 = (bf16[512,1024]{1,0:T(8,128)(2,1)S(1)}, bf16[512,1024]{1,0:T(8,128)(2,1)S(1)}, u32[]{:S(2)}, u32[]{:S(2)}) collective-permute-start(bf16[512,1024]{1,0:T(8,128)(2,1)S(1)} %pad_maximum_fusion.1), channel_id=1, source_target_pairs={{0,1},{1,0},{2,3},{3,2},{4,5},{5,4},{6,7},{7,6},{8,9},{9,8},{10,11... | collective-permute-start | bytes 3145736 | tf_op jit(solution)/shard_map/gather/ppermute | solution.py:16
  64.9 2.2 copy-start
  74.8 30.4 %all-to-all-start = ((f32[16,5,1024]{2,1,0:T(8,128)}), f32[16,5,1024]{2,1,0:T(8,128)S(1)}, u32[]{:S(2)}, u32[]{:S(2)}) async-start(f32[16,5,1024]{2,1,0:T(8,128)} %broadcast_in_dim.26), calls=%async_computation | async-start | bytes 1048576 | tf_op jit(solution)/shard_map/global_stats/all_to_all | solution.py:84
  82.5 92.5 %all-gather.5.cloned.1.call-start = ((), (), s32[]{:S(2)}) async-start(), calls=%async_computation.5 | async-start | bytes 2359296 | tf_op jit(solution)/shard_map/slope/all_gather | solution.py:134
  123.0 6.6 %collective-permute-start.3 = (bf16[128,1024]{1,0:T(8,128)(2,1)}, bf16[128,1024]{1,0:T(8,128)(2,1)S(1)}, u32[]{:S(2)}, u32[]{:S(2)}) collective-permute-start(bf16[128,1024]{1,0:T(8,128)(2,1)} %reduce-scatter.3.cloned.1.call-done), channel_id=1, source_target_pairs={{0,32},{32,0},{1,33},{33,1},{2,34},{34,2},{3,35},{35,3},{4,36},{36... | collective-permute-start | bytes 786440 | tf_op jit(solution)/shard_map/corr/ppermute | solution.py:16
  132.1 96.7 %reduce-scatter.5.cloned.1.call-start = ((), (), s32[]{:S(2)}) async-start(), calls=%async_computation.6 | async-start | bytes 2621440 | tf_op jit(solution)/shard_map/reduce/reduce_scatter | solution.py:177
  135.7 41.8 %copy-start.3 = (bf16[1024,1024]{1,0:T(8,128)(2,1)S(1)}, bf16[1024,1024]{1,0:T(8,128)(2,1)}, u32[]{:S(2)}) copy-start(bf16[1024,1024]{1,0:T(8,128)(2,1)} %copy-done.2) | copy-start | bytes 6291460
  137.5 4.2 %collective-permute-start.4 = (f32[5,1024]{1,0:T(8,128)S(1)}, f32[5,1024]{1,0:T(8,128)S(1)}, u32[]{:S(2)}, u32[]{:S(2)}) collective-permute-start(f32[5,1024]{1,0:T(8,128)S(1)} %concatenate.11), channel_id=1, source_target_pairs={{0,32},{32,0},{1,33},{33,1},{2,34},{34,2},{3,35},{35,3},{4,36},{36... | collective-permute-start | bytes 61448 | tf_op jit(solution)/shard_map/small_sums/ppermute | solution.py:23
  141.7 4.2 %collective-permute-start.5 = (f32[5,1024]{1,0:T(8,128)S(1)}, f32[5,1024]{1,0:T(8,128)S(1)}, u32[]{:S(2)}, u32[]{:S(2)}) collective-permute-start(f32[5,1024]{1,0:T(8,128)S(1)} %add.139), channel_id=1, source_target_pairs={{0,4},{4,0},{8,12},{12,8},{16,20},{20,16},{24,28},{28,24},{1,5},{5... | collective-permute-start | bytes 61448 | tf_op jit(solution)/shard_map/small_sums/ppermute | solution.py:23
  145.9 5.9 %collective-permute-start.6 = (f32[5,1024]{1,0:T(8,128)S(1)}, f32[5,1024]{1,0:T(8,128)S(1)}, u32[]{:S(2)}, u32[]{:S(2)}) collective-permute-start(f32[5,1024]{1,0:T(8,128)S(1)} %add.140), channel_id=1, source_target_pairs={{0,8},{4,12},{8,0},{12,4},{16,24},{20,28},{24,16},{28,20},{1,9},{5... | collective-permute-start | bytes 61448 | tf_op jit(solution)/shard_map/small_sums/ppermute | solution.py:23
  151.8 8.3 %collective-permute-start.7 = (f32[5,1024]{1,0:T(8,128)S(1)}, f32[5,1024]{1,0:T(8,128)S(1)}, u32[]{:S(2)}, u32[]{:S(2)}) collective-permute-start(f32[5,1024]{1,0:T(8,128)S(1)} %add.141), channel_id=1, source_target_pairs={{0,16},{4,20},{8,24},{12,28},{16,0},{20,4},{24,8},{28,12},{1,17},{... | collective-permute-start | bytes 61448 | tf_op jit(solution)/shard_map/small_sums/ppermute | solution.py:23
  160.1 1.2 collective-permute-start.8
  161.4 5.0 %collective-permute-start.9 = (f32[1,128]{1,0:T(1,128)S(1)}, f32[1,128]{1,0:T(1,128)S(1)}, u32[]{:S(2)}, u32[]{:S(2)}) collective-permute-start(f32[1,128]{1,0:T(1,128)S(1)} %slice_add_fusion), channel_id=1, source_target_pairs={{0,2},{2,0},{1,3},{3,1},{4,6},{6,4},{5,7},{7,5},{8,10},{10,8},{9,1... | collective-permute-start | bytes 1544 | tf_op jit(solution)/shard_map/small_sums/ppermute | solution.py:23
  166.4 3.5 %collective-permute-start.10 = (f32[1,128]{1,0:T(1,128)S(1)}, f32[1,128]{1,0:T(1,128)S(1)}, u32[]{:S(2)}, u32[]{:S(2)}) collective-permute-start(f32[1,128]{1,0:T(1,128)S(1)} %add.144), channel_id=1, source_target_pairs={{0,64},{64,0},{128,192},{192,128},{1,65},{65,1},{129,193},{193,129... | collective-permute-start | bytes 1544 | tf_op jit(solution)/shard_map/small_sums/ppermute | solution.py:23
  170.0 5.0 %collective-permute-start.11 = (f32[1,128]{1,0:T(1,128)S(1)}, f32[1,128]{1,0:T(1,128)S(1)}, u32[]{:S(2)}, u32[]{:S(2)}) collective-permute-start(f32[1,128]{1,0:T(1,128)S(1)} %add.145), channel_id=1, source_target_pairs={{0,128},{64,192},{128,0},{192,64},{1,129},{65,193},{129,1},{193,65... | collective-permute-start | bytes 1544 | tf_op jit(solution)/shard_map/small_sums/ppermute | solution.py:23
  177.6 6.2 %copy-start.5 = (bf16[1024,1024]{1,0:T(8,128)(2,1)S(1)}, bf16[1024,1024]{1,0:T(8,128)(2,1)}, u32[]{:S(2)}) copy-start(bf16[1024,1024]{1,0:T(8,128)(2,1)} %copy-done.4) | copy-start | bytes 6291460
  177.6 6.1 %copy-start.7 = (bf16[1024,1024]{1,0:T(8,128)(2,1)S(1)}, bf16[1024,1024]{1,0:T(8,128)(2,1)}, u32[]{:S(2)}) copy-start(bf16[1024,1024]{1,0:T(8,128)(2,1)} %all-gather.5.cloned.1.call-done) | copy-start | bytes 6291460
  189.3 2.7 %collective-permute-start.12 = (bf16[2,256,1024]{2,1,0:T(8,128)(2,1)S(1)}, bf16[2,256,1024]{2,1,0:T(8,128)(2,1)S(1)}, u32[]{:S(2)}, u32[]{:S(2)}) collective-permute-start(bf16[2,256,1024]{2,1,0:T(8,128)(2,1)S(1)} %select_bitcast_fusion), channel_id=1, source_target_pairs={{0,1},{1,0},{2,3},{3,2},{4,5},{5,4},{6,7},{7,6},{8,9},{9,8},{10,11... | collective-permute-start | bytes 3145736 | tf_op jit(solution)/shard_map/reduce/ppermute | solution.py:16
  192.8 15.6 %collective-permute-start.13 = (bf16[256,1024]{1,0:T(8,128)(2,1)S(1)}, bf16[256,1024]{1,0:T(8,128)(2,1)S(1)}, u32[]{:S(2)}, u32[]{:S(2)}) collective-permute-start(bf16[256,1024]{1,0:T(8,128)(2,1)S(1)} %fusion.33), channel_id=1, source_target_pairs={{0,2},{2,0},{1,3},{3,1},{4,6},{6,4},{5,7},{7,5},{8,10},{10,8},{9,1... | collective-permute-start | bytes 1572872 | tf_op jit(solution)/shard_map/reduce/ppermute | solution.py:16
  208.6 20.1 %collective-permute-start.14 = (bf16[256,1024]{1,0:T(8,128)(2,1)S(1)}, bf16[256,1024]{1,0:T(8,128)(2,1)S(1)}, u32[]{:S(2)}, u32[]{:S(2)}) collective-permute-start(bf16[256,1024]{1,0:T(8,128)(2,1)S(1)} %fusion.30), channel_id=1, source_target_pairs={{0,0},{1,64},{2,128},{3,192},{64,1},{65,65},{66,129},{67,193},{128... | collective-permute-start | bytes 1572872 | tf_op jit(solution)/shard_map/reduce/ppermute | solution.py:30
  (4 other events, 5.9 us)
Sparse Core Ops, SparseCore 0:
  27.7 37.1 all-gather.2
  71.1 51.8 reduce-scatter.2
  132.2 41.0 all-gather.4
  187.8 31.4 reduce-scatter.4

commit v3 on v2

--- a/solution.py
+++ b/solution.py
@@ -1,6 +1,10 @@
+import functools
+
 import jax
 import jax.numpy as jnp
 from jax import lax
+from jax.experimental import pallas as pl
+from jax.experimental.pallas import tpu as pltpu
 from jax.sharding import Mesh, PartitionSpec as P
 
 off_weight = 0.0051
@@ -28,6 +32,129 @@
 def transpose_blocks(value):
     pairs = [(g * 4 + f, f * 4 + g) for g in range(4) for f in range(4)]
     return lax.ppermute(value, PLANE, pairs)
+
+
+PARAMS = pltpu.CompilerParams(vmem_limit_bytes=48 * 1024 * 1024)
+
+
+def corr_kernel(order_ref, a_ref, b0_ref, b1_ref, b2_ref, b3_ref, out_ref, mean_ref, ca_ref, cb_ref):
+    rows = b0_ref.shape[0]
+    count = 4 * rows
+    width = out_ref.shape[1]
+    pieces = (b0_ref, b1_ref, b2_ref, b3_ref)
+    ones = jnp.ones((16, rows), bf16)
+    sum_a = jnp.zeros((16, width), f32)
+    sum_b = jnp.zeros((16, width), f32)
+    for place, piece in enumerate(pieces):
+        sum_a += jnp.dot(ones, a_ref[place], preferred_element_type=f32)
+        sum_b += jnp.dot(ones, piece[...], preferred_element_type=f32)
+    mean_a = sum_a[:1] / count
+    mean_b = sum_b[:1] / count
+    mean_ref[0:1] = mean_a
+    mean_ref[1:2] = mean_b
+    for place, piece in enumerate(pieces):
+        part = slice(place * rows, (place + 1) * rows)
+        ca_ref[part] = (a_ref[order_ref[place]].astype(f32) - mean_a).astype(bf16)
+        cb_ref[part] = (piece[...].astype(f32) - mean_b).astype(bf16)
+    chunk = min(256, width)
+    for start in range(0, width, chunk):
+        part = slice(start, start + chunk)
+        out_ref[part] = lax.dot_general(
+            ca_ref[:, part], cb_ref[...], (((0,), (0,)), ((), ())), preferred_element_type=f32
+        ).astype(bf16)
+
+
+def corr_call(order, block_a, pieces):
+    rows, width = pieces[0].shape
+    whole = pl.BlockSpec(memory_space=pltpu.VMEM)
+    return pl.pallas_call(
+        corr_kernel,
+        out_shape=(
+            jax.ShapeDtypeStruct((width, width), bf16),
+            jax.ShapeDtypeStruct((2, width), f32),
+        ),
+        in_specs=[pl.BlockSpec(memory_space=pltpu.SMEM)] + [whole] * 5,
+        out_specs=(whole, whole),
+        scratch_shapes=[pltpu.VMEM((4 * rows, width), bf16)] * 2,
+        compiler_params=PARAMS,
+        cost_estimate=pl.CostEstimate(
+            flops=8 * rows * width * width, bytes_accessed=24 * rows * width, transcendentals=0
+        ),
+        name="corr",
+    )(order, block_a.reshape(4, rows, width), *pieces)
+
+
+def back_rows(dims, left_ref, slope_ref, plain_ref, centre_ref, vec_ref):
+    slope = slope_ref[...]
+    back = lax.dot_general(left_ref[...], slope, dims, preferred_element_type=f32)
+    one = lax.dot_general(centre_ref[...], slope, dims, preferred_element_type=f32)
+    one = one[0:1] + one[1:2]
+    return (back - one - plain_ref[...].astype(f32) * vec_ref[0:1]) * vec_ref[1:2]
+
+
+AS_IS = (((1,), (0,)), ((), ()))
+TURNED = (((1,), (1,)), ((), ()))
+
+
+def back_kernel(dims, order_ref, left_ref, slope_ref, plain_ref, centre_ref, vec_ref, out_ref):
+    out_ref[...] = back_rows(dims, left_ref, slope_ref, plain_ref, centre_ref, vec_ref).astype(bf16)
+
+
+def keep_kernel(
+    dims, order_ref, left_ref, slope_ref, plain_ref, centre_ref, vec_ref, got_ref, send_ref, mine_ref
+):
+    value = back_rows(dims, left_ref, slope_ref, plain_ref, centre_ref, vec_ref)
+    value = value + got_ref[...].astype(f32)
+    step = pl.program_id(0)
+
+    @pl.when(step == 0)
+    def _():
+        send_ref[...] = value.astype(bf16)
+
+    @pl.when(step == 1)
+    def _():
+        mine_ref[...] = value
+
+
+def back_call(dims, order, steps, rows, left, slope, plain, centre, vec, got=None):
+    width = slope.shape[0]
+    picked = pl.BlockSpec((rows, width), lambda i, order: (order[i], 0))
+    fixed = lambda height: pl.BlockSpec((height, width), lambda i, order: (0, 0))
+    in_specs = [picked, fixed(width), picked, fixed(16), fixed(2)]
+    args = [left, slope, plain, centre, vec]
+    if got is None:
+        kernel = back_kernel
+        out_shape = jax.ShapeDtypeStruct((steps * rows, width), bf16)
+        out_specs = pl.BlockSpec((rows, width), lambda i, order: (i, 0))
+    else:
+        kernel = keep_kernel
+        in_specs.append(pl.BlockSpec((rows, width), lambda i, order: (order[2 + i], 0)))
+        args.append(got)
+        out_shape = (
+            jax.ShapeDtypeStruct((rows, width), bf16),
+            jax.ShapeDtypeStruct((rows, width), f32),
+        )
+        out_specs = (fixed(rows), fixed(rows))
+    return pl.pallas_call(
+        functools.partial(kernel, dims),
+        out_shape=out_shape,
+        grid_spec=pltpu.PrefetchScalarGridSpec(
+            num_scalar_prefetch=1, grid=(steps,), in_specs=in_specs, out_specs=out_specs
+        ),
+        compiler_params=PARAMS,
+        cost_estimate=pl.CostEstimate(
+            flops=2 * steps * rows * width * width,
+            bytes_accessed=6 * steps * rows * width + 2 * width * width,
+            transcendentals=0,
+        ),
+        name="back",
+    )(order, *args)
+
+
+def split_rows(row):
+    high = row.astype(bf16)
+    low = (row - high.astype(f32)).astype(bf16)
+    return jnp.concatenate([high[None], low[None], jnp.zeros((14, row.shape[0]), bf16)], 0)
 
 
 def on_device(embed_a, embed_b):
@@ -43,47 +170,43 @@
         block_a = lax.all_gather(embed_a, "y", axis=0, tiled=True)
         mine = transpose_blocks(embed_b)
         theirs = swap(mine, "xh")
-        pair = jnp.concatenate(
-            [jnp.where(xh == 0, mine, theirs), jnp.where(xh == 0, theirs, mine)], 0
-        )
-        other = swap(pair, "co")
-        even = jnp.where(co == 0, pair, other)
-        odd = jnp.where(co == 0, other, pair)
-        block_b = lax.optimization_barrier(
-            jnp.concatenate([even[:rows], odd[:rows], even[rows:], odd[rows:]], 0)
-        )
+        mine_other = swap(mine, "co")
+        theirs, block_a = lax.optimization_barrier((theirs, block_a))
+        theirs_other = swap(theirs, "co")
+        pieces = (mine, theirs, mine_other, theirs_other)
+        order = jnp.stack(
+            [2 * xh + co, 2 * (1 - xh) + co, 2 * xh + 1 - co, 2 * (1 - xh) + 1 - co]
+        ).astype(jnp.int32)
+
+    with jax.named_scope("corr"):
+        product, local = corr_call(order, block_a, pieces)
+        summed = lax.psum_scatter(product, "z", scatter_dimension=0, tiled=True)
+        piece = summed.astype(f32) + swap(summed, "xl").astype(f32)
 
     with jax.named_scope("local_stats"):
+        pieces, local = lax.optimization_barrier((pieces, local))
+        low = jnp.where(co == 0, jnp.stack(pieces[:2]), jnp.stack(pieces[2:]))
+        high = jnp.where(co == 0, jnp.stack(pieces[2:]), jnp.stack(pieces[:2]))
+        even = jnp.where(xh == 0, low, low[::-1])
+        odd = jnp.where(xh == 0, high, high[::-1])
+        block_b = jnp.stack([even[0], odd[0], even[1], odd[1]]).reshape(group_rows, width)
+        block_b = lax.optimization_barrier(block_b)
         value_a = block_a.astype(f32)
         value_b = block_b.astype(f32)
-        local_a = jnp.sum(value_a, 0) / group_rows
-        local_b = jnp.sum(value_b, 0) / group_rows
-        cent_a = value_a - local_a
-        cent_b = value_b - local_b
+        cent_a = value_a - local[0]
+        cent_b = value_b - local[1]
         stats = jnp.stack(
             [
-                local_a,
+                local[0],
                 jnp.sum(cent_a * cent_a, 0),
-                local_b,
+                local[1],
                 jnp.sum(cent_b * cent_b, 0),
                 jnp.sum(cent_a * cent_b, 0),
             ]
         )
 
-    with jax.named_scope("corr"):
-        product = lax.dot_general(
-            cent_a.astype(bf16),
-            cent_b.astype(bf16),
-            (((0,), (0,)), ((), ())),
-            preferred_element_type=f32,
-        ).astype(bf16)
-        summed = lax.psum_scatter(product, "z", scatter_dimension=0, tiled=True)
-        piece = summed.astype(f32) + swap(summed, "xl").astype(f32)
-
     with jax.named_scope("global_stats"):
-        every = lax.all_to_all(
-            jnp.broadcast_to(stats, (parts,) + stats.shape), BATCH, 0, 0, tiled=True
-        )
+        every = lax.all_gather(stats, BATCH)
         mean_a = jnp.sum(every[:, 0], 0) / parts
         mean_b = jnp.sum(every[:, 2], 0) / parts
         shift_a = every[:, 0] - mean_a
@@ -161,27 +284,25 @@
         two_a = small[2]
         two_b = small[3]
 
+        vec_a = jnp.stack([two_a, scale_a])
+        vec_b = jnp.stack([two_b, scale_b])
+        centre_a = split_rows(centre_a)
+        centre_b = split_rows(centre_b)
+
     with jax.named_scope("back"):
-        wide = slope.astype(f32)
-        one_a = jnp.sum(wide * centre_b, 1)
-        one_b = jnp.sum(wide * centre_a.reshape(width, 1), 0)
-        back_b = jnp.dot(norm_a, slope, preferred_element_type=f32)
-        part_b = ((back_b - one_b - plain_b * two_b) * scale_b).astype(bf16)
-        part_b, norm_b, slope = lax.optimization_barrier((part_b, norm_b, slope))
-        back_a = lax.dot_general(
-            norm_b, slope, (((1,), (1,)), ((), ())), preferred_element_type=f32
-        )
-        part_a = ((back_a - one_a - plain_a * two_a) * scale_a).astype(bf16)
-
-    with jax.named_scope("reduce"):
+        order = jnp.stack([1 - co, 3 - co]).astype(jnp.int32)
+        sent = back_call(AS_IS, order, 2, rows, norm_a, slope, norm_b, centre_a, vec_b)
+        received = swap(sent, "co")
+        slope, sent = lax.optimization_barrier((slope, sent))
+        order = jnp.arange(4, dtype=jnp.int32)
+        part_a = back_call(TURNED, order, 4, rows, norm_b, slope, norm_a, centre_b, vec_a)
         grad_a = lax.psum_scatter(part_a, "y", scatter_dimension=0, tiled=True)
-        quarters = part_b.reshape(2, 2, rows, width)
-        even, odd = quarters[:, 0], quarters[:, 1]
-        received = swap(jnp.where(co == 0, odd, even), "co")
-        pair = jnp.where(co == 0, even, odd).astype(f32) + received.astype(f32)
-        received = swap(jnp.where(xh == 0, pair[1], pair[0]).astype(bf16), "xh")
-        mine = jnp.where(xh == 0, pair[0], pair[1]) + received.astype(f32)
-        grad_b = transpose_blocks(mine.astype(bf16))
+        order = jnp.stack([2 * (1 - xh) + co, 2 * xh + co, 1 - xh, xh]).astype(jnp.int32)
+        sent, mine = back_call(
+            AS_IS, order, 2, rows, norm_a, slope, norm_b, centre_a, vec_b, received
+        )
+        received = swap(sent, "xh")
+        grad_b = transpose_blocks((mine + received.astype(f32)).astype(bf16))
     return (grad_a, grad_b, loss_mean)
 
 

time: 239 us -> 220 us (0.921)
  waiting for transfers between devices: 157 us -> 102 us
  blocking collectives: 0 us -> 41.4 us
  Pallas kernels: 0 us -> 22.6 us
  matrix products: 16.3 us -> 0.63 us
  starting transfers between devices: 29.6 us -> 20.3 us
  other arithmetic: 13.4 us -> 8.39 us
  local copies, waits for them, and re-layouts: 5.35 us -> 8.69 us
    all_gather x0 -> x1, blocking collectives: none -> 41.4 us  [on_device(): every = lax.all_gather(stats, BATCH)]
    pallas_call x0 -> x4, Pallas kernels: none -> 22.6 us  [the longest x3 16.4 us: back_call(): pl.pallas_call(functools.partial(kernel, dims), out_shape=out_shape, grid...]
    all_to_all x1 -> x0, waiting for transfers between devices: 22.6 us -> none  [on_device(): lax.all_to_all(jnp.broadcast_to(stats, (parts,) + stats.shape), BATCH, 0,...]
    reduce_scatter x1, waiting for transfers between devices: 17.4 us -> 0.02 us  [on_device(): summed = lax.psum_scatter(product, 'z', scatter_dimension=0, tiled=True)]
    all_gather x1, waiting for transfers between devices: 18.5 us -> 3.19 us  [on_device(): block_a = lax.all_gather(embed_a, 'y', axis=0, tiled=True)]
    dot_general x3 -> x0, matrix products: 13.8 us -> none  [the longest x1 6.13 us: on_device(): back_b = jnp.dot(norm_a, slope, preferred_element_type=f32)]
    all_to_all x1 -> x0, starting transfers between devices: 7.73 us -> none  [on_device(): lax.all_to_all(jnp.broadcast_to(stats, (parts,) + stats.shape), BATCH, 0,...]
    reduce_sum x3 -> x0, other arithmetic: 5.02 us -> none  [the longest x1 2.54 us: on_device(): one_b = jnp.sum(wide * centre_a.reshape(width, 1), 0)]
  transfers between devices with their start and end apart: 20 -> 20, of which waited for: 18 -> 16; matrix products, arithmetic and copies ran while one was open for 4% -> 3% of each run, Pallas kernels for 0% -> 2%
where the time goes in v3:
time: 220 us; the launch traced here: 219 us
  waiting for transfers between devices  102 us (46%)
  blocking collectives  41.4 us (19%)
  Pallas kernels  22.6 us (10%)
  starting transfers between devices  20.3 us (9%)
  between operations  15.8 us (7%)
  local copies, waits for them, and re-layouts  8.69 us (4%)
  other arithmetic  8.39 us (4%)
    all_gather x1, blocking collectives, on_device(): every = lax.all_gather(stats, BATCH)  41.4 us
    ppermute x6, waiting for transfers between devices, swap(): return lax.ppermute(value, axis, [(0, 1), (1, 0)])  38.5 us
    ppermute x8, waiting for transfers between devices, butterfly(): lax.ppermute(value, axis, [(i, i ^ step) for i in range(size)])  30.1 us
    ppermute x2, waiting for transfers between devices, transpose_blocks(): return lax.ppermute(value, PLANE, pairs)  29 us
    pallas_call x3, Pallas kernels, back_call(): pl.pallas_call(functools.partial(kernel, dims), out_shape=out_shape, grid...  16.4 us
    ppermute x2, starting transfers between devices, transpose_blocks(): return lax.ppermute(value, PLANE, pairs)  11.3 us
    unnamed x19, local copies, waits for them, and re-layouts  8.27 us
    ppermute x8, starting transfers between devices, butterfly(): lax.ppermute(value, axis, [(i, i ^ step) for i in range(size)])  6.68 us
  transfers between devices with their start and end apart: 20, of which 16 were waited for; matrix products, arithmetic and copies ran while one was open for 3% of the time, Pallas kernels for 2%

profile of v3, /device:TPU:4, one launch (start us, length us, event | category | flops | bytes accessed | tf_op | source)
XLA Modules:
  0.0 219.5 jit_solution(4032482236673524626)
XLA Ops:
  7.9 5.0 %collective-permute-start = (bf16[256,1024]{1,0:T(8,128)(2,1)}, bf16[256,1024]{1,0:T(8,128)(2,1)S(1)}, u32[]{:S(2)}, u32[]{:S(2)}) collective-permute-start(bf16[256,1024]{1,0:T(8,128)(2,1)} %param.3), channel_id=1, source_target_pairs={{0,0},{1,64},{2,128},{3,192},{64,1},{65,65},{66,129},{67,193},{128... | collective-permute-start | bytes 1572872 | tf_op jit(solution)/shard_map/gather/ppermute | solution.py:34
  13.0 15.3 %collective-permute-done.b0_ref = bf16[256,1024]{1,0:T(8,128)(2,1)S(1)} collective-permute-done((bf16[256,1024]{1,0:T(8,128)(2,1)}, bf16[256,1024]{1,0:T(8,128)(2,1)S(1)}, u32[]{:S(2)}, u32[]{:S(2)}) %collective-permute-start) | collective-permute-done | bytes 524320 | tf_op jit(solution)/shard_map/gather/ppermute | solution.py:34
  28.3 14.7 %collective-permute-done.1.b1_ref = bf16[256,1024]{1,0:T(8,128)(2,1)S(1)} collective-permute-done((bf16[256,1024]{1,0:T(8,128)(2,1)S(1)}, bf16[256,1024]{1,0:T(8,128)(2,1)S(1)}, u32[]{:S(2)}, u32[]{:S(2)}) %collective-permute-start.1) | collective-permute-done | bytes 524320 | tf_op jit(solution)/shard_map/gather/ppermute | solution.py:20
  43.0 3.2 %all-gather.5.cloned.1.call-done = bf16[1024,1024]{1,0:T(8,128)(2,1)} async-done(((bf16[256,1024]{1,0:T(8,128)(2,1)}), bf16[1024,1024]{1,0:T(8,128)(2,1)}) %all-gather.5.cloned.1.call-update) | async-done | bytes 2097168 | tf_op jit(solution)/shard_map/gather/all_gather | solution.py:170
  48.1 6.2 %corr.1 = (bf16[1024,1024]{1,0:T(8,128)(2,1)}, f32[2,1024]{1,0:T(2,128)S(1)}) custom-call(s32[4]{0:T(128)S(1)} %pad_add_fusion.order_ref, bf16[4,256,1024]{2,1,0:T(8,128)(2,1)} %bitcast.47, bf16[256,1024]{1,0:T(8,128)(2,1)S(1)} %collective-permute-done.b0_ref, bf16[256,1024]{1,0:T(8,128)(2,1)S(1)} %collective-permute-done.1.b1_ref, ...), custom_call_target="tpu_custom_call" | custom-call | flops 2147483648 | bytes 6291456 | tf_op jit(solution)/shard_map/corr/corr/pallas_call | solution.py:70
  58.4 41.4 %all-gather.1 = f32[16,5,1024]{2,1,0:T(8,128)S(1)} all-gather(f32[1,5,1024]{2,1,0:T(8,128)S(1)} %bitcast.48), channel_id=2, replica_groups=mesh['y'=4,'xl'=2,'z'=8,'xh'=2,'co'=2] {'xl','z'}, dimensions={0}, use_global_device_ids=true | all-gather | bytes 348160 | tf_op jit(solution)/shard_map/global_stats/all_gather | solution.py:209
  101.7 5.3 %collective-permute-done.4 = bf16[128,1024]{1,0:T(8,128)(2,1)S(1)} collective-permute-done((bf16[128,1024]{1,0:T(8,128)(2,1)}, bf16[128,1024]{1,0:T(8,128)(2,1)S(1)}, u32[]{:S(2)}, u32[]{:S(2)}) %collective-permute-start.4) | collective-permute-done | bytes 262176 | tf_op jit(solution)/shard_map/corr/ppermute | solution.py:20
  107.0 2.2 fusion.15
  115.2 3.3 %collective-permute-done.5 = f32[5,1024]{1,0:T(8,128)S(1)} collective-permute-done((f32[5,1024]{1,0:T(8,128)S(1)}, f32[5,1024]{1,0:T(8,128)S(1)}, u32[]{:S(2)}, u32[]{:S(2)}) %collective-permute-start.5) | collective-permute-done | bytes 20512 | tf_op jit(solution)/shard_map/small_sums/ppermute | solution.py:27
  118.6 4.5 %collective-permute-done.6 = f32[5,1024]{1,0:T(8,128)S(1)} collective-permute-done((f32[5,1024]{1,0:T(8,128)S(1)}, f32[5,1024]{1,0:T(8,128)S(1)}, u32[]{:S(2)}, u32[]{:S(2)}) %collective-permute-start.6) | collective-permute-done | bytes 20512 | tf_op jit(solution)/shard_map/small_sums/ppermute | solution.py:27
  123.1 5.1 %collective-permute-done.7 = f32[5,1024]{1,0:T(8,128)S(1)} collective-permute-done((f32[5,1024]{1,0:T(8,128)S(1)}, f32[5,1024]{1,0:T(8,128)S(1)}, u32[]{:S(2)}, u32[]{:S(2)}) %collective-permute-start.7) | collective-permute-done | bytes 20512 | tf_op jit(solution)/shard_map/small_sums/ppermute | solution.py:27
  128.2 2.2 collective-permute-start.8
  130.4 6.2 %collective-permute-done.8 = f32[5,1024]{1,0:T(8,128)S(1)} collective-permute-done((f32[5,1024]{1,0:T(8,128)S(1)}, f32[5,1024]{1,0:T(8,128)S(1)}, u32[]{:S(2)}, u32[]{:S(2)}) %collective-permute-start.8) | collective-permute-done | bytes 20512 | tf_op jit(solution)/shard_map/small_sums/ppermute | solution.py:27
  138.1 4.7 %collective-permute-done.10 = f32[1,128]{1,0:T(1,128)S(1)} collective-permute-done((f32[1,128]{1,0:T(1,128)S(1)}, f32[1,128]{1,0:T(1,128)S(1)}, u32[]{:S(2)}, u32[]{:S(2)}) %collective-permute-start.10) | collective-permute-done | bytes 544 | tf_op jit(solution)/shard_map/small_sums/ppermute | solution.py:27
  143.9 2.5 %collective-permute-done.11 = f32[1,128]{1,0:T(1,128)S(1)} collective-permute-done((f32[1,128]{1,0:T(1,128)S(1)}, f32[1,128]{1,0:T(1,128)S(1)}, u32[]{:S(2)}, u32[]{:S(2)}) %collective-permute-start.11) | collective-permute-done | bytes 544 | tf_op jit(solution)/shard_map/small_sums/ppermute | solution.py:27
  146.4 2.2 %collective-permute-start.12 = (f32[1,128]{1,0:T(1,128)S(1)}, f32[1,128]{1,0:T(1,128)S(1)}, u32[]{:S(2)}, u32[]{:S(2)}) collective-permute-start(f32[1,128]{1,0:T(1,128)S(1)} %add.181), channel_id=1, source_target_pairs={{0,128},{64,192},{128,0},{192,64},{1,129},{65,193},{129,1},{193,65... | collective-permute-start | bytes 1544 | tf_op jit(solution)/shard_map/small_sums/ppermute | solution.py:27
  148.7 2.7 %collective-permute-done.12 = f32[1,128]{1,0:T(1,128)S(1)} collective-permute-done((f32[1,128]{1,0:T(1,128)S(1)}, f32[1,128]{1,0:T(1,128)S(1)}, u32[]{:S(2)}, u32[]{:S(2)}) %collective-permute-start.12) | collective-permute-done | bytes 544 | tf_op jit(solution)/shard_map/small_sums/ppermute | solution.py:27
  154.7 3.8 %back.3 = bf16[512,1024]{1,0:T(8,128)(2,1)S(1)} custom-call(s32[2]{0:T(128)S(1)} %pad_add_fusion.1.order_ref, bf16[1024,1024]{1,0:T(8,128)(2,1)S(1)} %copy-done.3, bf16[1024,1024]{1,0:T(8,128)(2,1)S(1)} %copy-done.5, bf16[1024,1024]{1,0:T(8,128)(2,1)} %copy-done, bf16[16,1024]{1,0:T(8,128)(2,1)S(1)} %get-tuple-element.79.centre_ref, ...), custom_call_target="tpu_custom_call" | custom-call | flops 1073741824 | bytes 5242880 | tf_op jit(solution)/shard_map/back/back/pallas_call | solution.py:138
  158.6 7.9 %back.4 = bf16[1024,1024]{1,0:T(8,128)(2,1)S(1)} custom-call(s32[4]{0:T(128)S(1)} %iota.14.order_ref, bf16[1024,1024]{1,0:T(8,128)(2,1)S(1)} %copy-done.1, bf16[1024,1024]{1,0:T(8,128)(2,1)} %all-gather.7.cloned.1.call-done.slope_ref, bf16[1024,1024]{1,0:T(8,128)(2,1)} %copy-done.2, bf16[16,1024]{1,0:T(8,128)(2,1)S(1)} %get-tuple-element.78.centre_ref, ...), custom_call_target="tpu_custom_call" | custom-call | flops 2147483648 | bytes 8388608 | tf_op jit(solution)/shard_map/back/back/pallas_call | solution.py:138
  168.1 2.6 %collective-permute-done.13.got_ref = bf16[512,1024]{1,0:T(8,128)(2,1)S(1)} collective-permute-done((bf16[512,1024]{1,0:T(8,128)(2,1)S(1)}, bf16[512,1024]{1,0:T(8,128)(2,1)S(1)}, u32[]{:S(2)}, u32[]{:S(2)}) %collective-permute-start.13) | collective-permute-done | bytes 1048608 | tf_op jit(solution)/shard_map/back/ppermute | solution.py:20
  170.6 4.7 %back.5 = (bf16[256,1024]{1,0:T(8,128)(2,1)S(1)}, f32[256,1024]{1,0:T(8,128)S(1)}) custom-call(s32[4]{0:T(128)S(1)} %pad_add_fusion.2.order_ref, bf16[1024,1024]{1,0:T(8,128)(2,1)S(1)} %copy-done.4, bf16[1024,1024]{1,0:T(8,128)(2,1)} %all-gather.7.cloned.1.call-done.slope_ref, bf16[1024,1024]{1,0:T(8,128)(2,1)} %copy-done, ...), custom_call_target="tpu_custom_call" | custom-call | flops 1073741824 | bytes 5242880 | tf_op jit(solution)/shard_map/back/back/pallas_call | solution.py:138
  176.8 14.1 %collective-permute-done.14 = bf16[256,1024]{1,0:T(8,128)(2,1)S(1)} collective-permute-done((bf16[256,1024]{1,0:T(8,128)(2,1)S(1)}, bf16[256,1024]{1,0:T(8,128)(2,1)S(1)}, u32[]{:S(2)}, u32[]{:S(2)}) %collective-permute-start.14) | collective-permute-done | bytes 524320 | tf_op jit(solution)/shard_map/back/ppermute | solution.py:20
  191.1 6.2 %collective-permute-start.15 = (bf16[256,1024]{1,0:T(8,128)(2,1)S(1)}, bf16[256,1024]{1,0:T(8,128)(2,1)S(1)}, u32[]{:S(2)}, u32[]{:S(2)}) collective-permute-start(bf16[256,1024]{1,0:T(8,128)(2,1)S(1)} %add_convert_fusion), channel_id=1, source_target_pairs={{0,0},{1,64},{2,128},{3,192},{64,1},{65,65},{66,129},{67,193},{128... | collective-permute-start | bytes 1572872 | tf_op jit(solution)/shard_map/back/ppermute | solution.py:34
  197.3 13.7 %collective-permute-done.15 = bf16[256,1024]{1,0:T(8,128)(2,1)S(1)} collective-permute-done((bf16[256,1024]{1,0:T(8,128)(2,1)S(1)}, bf16[256,1024]{1,0:T(8,128)(2,1)S(1)}, u32[]{:S(2)}, u32[]{:S(2)}) %collective-permute-start.15) | collective-permute-done | bytes 524320 | tf_op jit(solution)/shard_map/back/ppermute | solution.py:34
  (91 shorter events, 23.9 us)
Async XLA Ops:
  7.2 39.0 %all-gather.5.cloned.1.call-start = ((), (), s32[]{:S(2)}) async-start(), calls=%async_computation.2 | async-start | bytes 2621440 | tf_op jit(solution)/shard_map/gather/all_gather | solution.py:170
  7.9 92.4 %reduce-scatter.3.cloned.1.call-start = ((), (), s32[]{:S(2)}) async-start(), calls=%async_computation.3 | async-start | bytes 2359296 | tf_op jit(solution)/shard_map/corr/reduce_scatter | solution.py:183
  7.9 20.3 %collective-permute-start = (bf16[256,1024]{1,0:T(8,128)(2,1)}, bf16[256,1024]{1,0:T(8,128)(2,1)S(1)}, u32[]{:S(2)}, u32[]{:S(2)}) collective-permute-start(bf16[256,1024]{1,0:T(8,128)(2,1)} %param.3), channel_id=1, source_target_pairs={{0,0},{1,64},{2,128},{3,192},{64,1},{65,65},{66,129},{67,193},{128... | collective-permute-start | bytes 1572872 | tf_op jit(solution)/shard_map/gather/ppermute | solution.py:34
  28.3 14.7 %collective-permute-start.1 = (bf16[256,1024]{1,0:T(8,128)(2,1)S(1)}, bf16[256,1024]{1,0:T(8,128)(2,1)S(1)}, u32[]{:S(2)}, u32[]{:S(2)}) collective-permute-start(bf16[256,1024]{1,0:T(8,128)(2,1)S(1)} %collective-permute-done.b0_ref), channel_id=1, source_target_pairs={{0,2},{2,0},{1,3},{3,1},{4,6},{6,4},{5,7},{7,5},{8,10},{10,8},{9,1... | collective-permute-start | bytes 1572872 | tf_op jit(solution)/shard_map/gather/ppermute | solution.py:20
  28.3 18.0 %collective-permute-start.2 = (bf16[256,1024]{1,0:T(8,128)(2,1)S(1)}, bf16[256,1024]{1,0:T(8,128)(2,1)S(1)}, u32[]{:S(2)}, u32[]{:S(2)}) collective-permute-start(bf16[256,1024]{1,0:T(8,128)(2,1)S(1)} %collective-permute-done.b0_ref), channel_id=1, source_target_pairs={{0,1},{1,0},{2,3},{3,2},{4,5},{5,4},{6,7},{7,6},{8,9},{9,8},{10,11... | collective-permute-start | bytes 1572872 | tf_op jit(solution)/shard_map/gather/ppermute | solution.py:20
  46.2 1.9 collective-permute-start.3
  54.3 97.1 %all-gather.7.cloned.1.call-start = ((), (), s32[]{:S(2)}) async-start(), calls=%async_computation.4 | async-start | bytes 2359296 | tf_op jit(solution)/shard_map/slope/all_gather | solution.py:257
  55.4 1.6 copy-start.7
  100.3 6.7 %collective-permute-start.4 = (bf16[128,1024]{1,0:T(8,128)(2,1)}, bf16[128,1024]{1,0:T(8,128)(2,1)S(1)}, u32[]{:S(2)}, u32[]{:S(2)}) collective-permute-start(bf16[128,1024]{1,0:T(8,128)(2,1)} %reduce-scatter.3.cloned.1.call-done), channel_id=1, source_target_pairs={{0,32},{32,0},{1,33},{33,1},{2,34},{34,2},{3,35},{35,3},{4,36},{36... | collective-permute-start | bytes 786440 | tf_op jit(solution)/shard_map/corr/ppermute | solution.py:20
  110.0 101.0 %reduce-scatter.5.cloned.1.call-start = ((), (), s32[]{:S(2)}) async-start(), calls=%async_computation.5 | async-start | bytes 2621440 | tf_op jit(solution)/shard_map/back/reduce_scatter | solution.py:299
  110.1 1.6 copy-start.8
  114.4 4.2 %collective-permute-start.5 = (f32[5,1024]{1,0:T(8,128)S(1)}, f32[5,1024]{1,0:T(8,128)S(1)}, u32[]{:S(2)}, u32[]{:S(2)}) collective-permute-start(f32[5,1024]{1,0:T(8,128)S(1)} %concatenate.9), channel_id=1, source_target_pairs={{0,32},{32,0},{1,33},{33,1},{2,34},{34,2},{3,35},{35,3},{4,36},{36... | collective-permute-start | bytes 61448 | tf_op jit(solution)/shard_map/small_sums/ppermute | solution.py:27
  118.6 4.5 %collective-permute-start.6 = (f32[5,1024]{1,0:T(8,128)S(1)}, f32[5,1024]{1,0:T(8,128)S(1)}, u32[]{:S(2)}, u32[]{:S(2)}) collective-permute-start(f32[5,1024]{1,0:T(8,128)S(1)} %add.175), channel_id=1, source_target_pairs={{0,4},{4,0},{8,12},{12,8},{16,20},{20,16},{24,28},{28,24},{1,5},{5... | collective-permute-start | bytes 61448 | tf_op jit(solution)/shard_map/small_sums/ppermute | solution.py:27
  123.1 5.1 %collective-permute-start.7 = (f32[5,1024]{1,0:T(8,128)S(1)}, f32[5,1024]{1,0:T(8,128)S(1)}, u32[]{:S(2)}, u32[]{:S(2)}) collective-permute-start(f32[5,1024]{1,0:T(8,128)S(1)} %add.176), channel_id=1, source_target_pairs={{0,8},{4,12},{8,0},{12,4},{16,24},{20,28},{24,16},{28,20},{1,9},{5... | collective-permute-start | bytes 61448 | tf_op jit(solution)/shard_map/small_sums/ppermute | solution.py:27
  128.2 8.3 %collective-permute-start.8 = (f32[5,1024]{1,0:T(8,128)S(1)}, f32[5,1024]{1,0:T(8,128)S(1)}, u32[]{:S(2)}, u32[]{:S(2)}) collective-permute-start(f32[5,1024]{1,0:T(8,128)S(1)} %add.177), channel_id=1, source_target_pairs={{0,16},{4,20},{8,24},{12,28},{16,0},{20,4},{24,8},{28,12},{1,17},{... | collective-permute-start | bytes 61448 | tf_op jit(solution)/shard_map/small_sums/ppermute | solution.py:27
  136.6 1.2 collective-permute-start.9
  137.8 5.0 %collective-permute-start.10 = (f32[1,128]{1,0:T(1,128)S(1)}, f32[1,128]{1,0:T(1,128)S(1)}, u32[]{:S(2)}, u32[]{:S(2)}) collective-permute-start(f32[1,128]{1,0:T(1,128)S(1)} %slice_add_fusion), channel_id=1, source_target_pairs={{0,2},{2,0},{1,3},{3,1},{4,6},{6,4},{5,7},{7,5},{8,10},{10,8},{9,1... | collective-permute-start | bytes 1544 | tf_op jit(solution)/shard_map/small_sums/ppermute | solution.py:27
  142.8 3.5 %collective-permute-start.11 = (f32[1,128]{1,0:T(1,128)S(1)}, f32[1,128]{1,0:T(1,128)S(1)}, u32[]{:S(2)}, u32[]{:S(2)}) collective-permute-start(f32[1,128]{1,0:T(1,128)S(1)} %add.180), channel_id=1, source_target_pairs={{0,64},{64,0},{128,192},{192,128},{1,65},{65,1},{129,193},{193,129... | collective-permute-start | bytes 1544 | tf_op jit(solution)/shard_map/small_sums/ppermute | solution.py:27
  146.4 5.0 %collective-permute-start.12 = (f32[1,128]{1,0:T(1,128)S(1)}, f32[1,128]{1,0:T(1,128)S(1)}, u32[]{:S(2)}, u32[]{:S(2)}) collective-permute-start(f32[1,128]{1,0:T(1,128)S(1)} %add.181), channel_id=1, source_target_pairs={{0,128},{64,192},{128,0},{192,64},{1,129},{65,193},{129,1},{193,65... | collective-permute-start | bytes 1544 | tf_op jit(solution)/shard_map/small_sums/ppermute | solution.py:27
  154.7 3.9 %copy-start.1 = (bf16[1024,1024]{1,0:T(8,128)(2,1)S(1)}, bf16[1024,1024]{1,0:T(8,128)(2,1)}, u32[]{:S(2)}) copy-start(bf16[1024,1024]{1,0:T(8,128)(2,1)} %copy-done) | copy-start | bytes 6291460
  167.8 2.8 %copy-start.4 = (bf16[1024,1024]{1,0:T(8,128)(2,1)S(1)}, bf16[1024,1024]{1,0:T(8,128)(2,1)}, u32[]{:S(2)}) copy-start(bf16[1024,1024]{1,0:T(8,128)(2,1)} %copy-done.2) | copy-start | bytes 6291460
  167.9 2.7 %collective-permute-start.13 = (bf16[512,1024]{1,0:T(8,128)(2,1)S(1)}, bf16[512,1024]{1,0:T(8,128)(2,1)S(1)}, u32[]{:S(2)}, u32[]{:S(2)}) collective-permute-start(bf16[512,1024]{1,0:T(8,128)(2,1)S(1)} %back.3), channel_id=1, source_target_pairs={{0,1},{1,0},{2,3},{3,2},{4,5},{5,4},{6,7},{7,6},{8,9},{9,8},{10,11... | collective-permute-start | bytes 3145736 | tf_op jit(solution)/shard_map/back/ppermute | solution.py:20
  175.3 15.6 %collective-permute-start.14 = (bf16[256,1024]{1,0:T(8,128)(2,1)S(1)}, bf16[256,1024]{1,0:T(8,128)(2,1)S(1)}, u32[]{:S(2)}, u32[]{:S(2)}) collective-permute-start(bf16[256,1024]{1,0:T(8,128)(2,1)S(1)} %get-tuple-element.35), channel_id=1, source_target_pairs={{0,2},{2,0},{1,3},{3,1},{4,6},{6,4},{5,7},{7,5},{8,10},{10,8},{9,1... | collective-permute-start | bytes 1572872 | tf_op jit(solution)/shard_map/back/ppermute | solution.py:20
  191.1 20.0 %collective-permute-start.15 = (bf16[256,1024]{1,0:T(8,128)(2,1)S(1)}, bf16[256,1024]{1,0:T(8,128)(2,1)S(1)}, u32[]{:S(2)}, u32[]{:S(2)}) collective-permute-start(bf16[256,1024]{1,0:T(8,128)(2,1)S(1)} %add_convert_fusion), channel_id=1, source_target_pairs={{0,0},{1,64},{2,128},{3,192},{64,1},{65,65},{66,129},{67,193},{128... | collective-permute-start | bytes 1572872 | tf_op jit(solution)/shard_map/back/ppermute | solution.py:34
  (5 other events, 7.2 us)
Sparse Core Ops, SparseCore 0:
  9.8 36.3 all-gather.4
  54.4 44.4 reduce-scatter.2
  110.2 39.6 all-gather.6
  168.0 30.3 reduce-scatter.4
